TPU v7x, 32 devices: a whole 2x2x4 slice. The times are simulated.
32 devices in a mesh: gx: 4 (over y, core), gy: 4 (over z), gz: 2 (over x).
Axes of the slice: x: 2, y: 2, z: 4, core: 2. Of those that a mesh axis runs over, the one named last changes fastest.
Arguments:
- density: float32 [32, 64, 4096], P('gz', 'gx', 'gy'), may hold values from 0.1 to 10
Outputs:
- details_one: float32 [7, 16, 32, 2048], P(None, 'gz', 'gx', 'gy')
- details_two: float32 [7, 8, 16, 1024], P(None, 'gz', 'gx', 'gy')
- details_three: float32 [7, 4, 8, 512], P(None, 'gz', 'gx', 'gy')
- approximation: float32 [4, 8, 512], P('gz', 'gx', 'gy')
All inputs are finite; a program needn't handle non-finite values.
Results may differ from a plain program's by a relative error of at most 0.00011.
Values sent between devices are 32-bit elements; how exact they have to be, the bound alone decides.
A program may use at most 128 MiB of HBM per device.

v0:
```python
import jax
import jax.numpy as jnp
from jax import lax
from jax.sharding import PartitionSpec as P

ALPHA = -1.586134342
BETA = -0.05298011854
GAMMA = 0.8829110762
DELTA = 0.4435068522
ZETA = 1.149604398


def padded_2(x, sides, width):
    for axis, dim in sides:
        peers, length = (lax.axis_size(axis), x.shape[dim])
        up = [(i, (i + 1) % peers) for i in range(peers)]
        down = [(j, i) for i, j in up]
        last = lax.slice_in_dim(x, length - width, length, axis=dim)
        initial = lax.slice_in_dim(x, 0, width, axis=dim)
        before = lax.ppermute(last, axis, up)
        after = lax.ppermute(initial, axis, down)
        x = jnp.concatenate([before, x, after], axis=dim)
    return x


def cut(values, start, stop, dim):
    return lax.slice_in_dim(values, start, stop, 1, dim)


def lift_padded(padded, dim):
    length = padded.shape[dim]
    half = length // 2 - 4
    paired = padded.reshape(padded.shape[:dim] + (length // 2, 2) + padded.shape[dim + 1 :])
    evens = lax.index_in_dim(paired, 0, dim + 1, False)
    odds = lax.index_in_dim(paired, 1, dim + 1, False)
    first_d = cut(odds, 0, half + 3, dim) + ALPHA * (
        cut(evens, 0, half + 3, dim) + cut(evens, 1, half + 4, dim)
    )
    first_s = cut(evens, 1, half + 3, dim) + BETA * (
        cut(first_d, 0, half + 2, dim) + cut(first_d, 1, half + 3, dim)
    )
    second_d = cut(first_d, 1, half + 2, dim) + GAMMA * (
        cut(first_s, 0, half + 1, dim) + cut(first_s, 1, half + 2, dim)
    )
    second_s = cut(first_s, 1, half + 1, dim) + DELTA * (
        cut(second_d, 0, half, dim) + cut(second_d, 1, half + 1, dim)
    )
    lower = second_s * ZETA
    upper = cut(second_d, 1, half + 1, dim) / ZETA
    return jnp.concatenate([lower, upper], axis=0)


def pad_remote(data, dim):
    if dim == 2:
        return padded_2(data, (("gx", 2),), 4)
    if dim == 3:
        return padded_2(data, (("gy", 3),), 4)
    return padded_2(data, (("gz", 1),), 4)


def spread_level(data):
    for dim in (2, 3, 1):
        data = lift_padded(pad_remote(data, dim), dim)
    return data


def on_device(density):
    first = spread_level(density[None])
    details_one = first[1:]
    coarse = first[0:1]
    second = spread_level(coarse)
    third = spread_level(second[0:1])
    details_two = second[1:]
    details_three = third[1:]
    approximation = third[0]
    return (details_one, details_two, details_three, approximation)


def solution(mesh):
    return jax.shard_map(
        on_device,
        mesh=mesh,
        in_specs=(P("gz", "gx", "gy"),),
        out_specs=(
            P(None, "gz", "gx", "gy"),
            P(None, "gz", "gx", "gy"),
            P(None, "gz", "gx", "gy"),
            P("gz", "gx", "gy"),
        ),
        check_vma=False,
    )
```

profile of v0, /device:TPU:0, one launch (start us, length us, event | category | flops | bytes accessed | tf_op | source)
XLA Modules:
  0.0 101.8 jit_solution(6678393170522309211)
XLA Ops:
  0.6 1.8 %copy.127 = f32[16,16,1024]{2,0,1:T(8,128)S(1)} copy(f32[16,16,1024]{2,1,0:T(8,128)} %param.1) | data formatting | bytes 2097152 | tf_op args[0]
  3.0 2.0 %collective-permute-start.1 = (f32[1,16,4,1024]{3,1,2,0:T(8,128)S(1)}, f32[1,16,4,1024]{3,1,2,0:T(8,128)S(1)}, u32[]{:S(2)}, u32[]{:S(2)}) collective-permute-start(f32[1,16,4,1024]{3,1,2,0:T(8,128)S(1)} %get-tuple-element.17), channel_id=1, source_target_pairs={{8,0},{16,8},{24,16},{0,24},{9,1},{17,9},{25,17},{1,25},{10,2},{18... | collective-permute-start | bytes 786440 | tf_op jit(solution)/shard_map/ppermute | solution.py:21
  5.0 4.1 %collective-permute-done = f32[1,16,4,1024]{3,1,2,0:T(8,128)S(1)} collective-permute-done((f32[1,16,4,1024]{3,1,2,0:T(8,128)S(1)}, f32[1,16,4,1024]{3,1,2,0:T(8,128)S(1)}, u32[]{:S(2)}, u32[]{:S(2)}) %collective-permute-start) | collective-permute-done | bytes 262176 | tf_op jit(solution)/shard_map/ppermute | solution.py:20
  9.2 2.5 %collective-permute-done.1 = f32[1,16,4,1024]{3,1,2,0:T(8,128)S(1)} collective-permute-done((f32[1,16,4,1024]{3,1,2,0:T(8,128)S(1)}, f32[1,16,4,1024]{3,1,2,0:T(8,128)S(1)}, u32[]{:S(2)}, u32[]{:S(2)}) %collective-permute-start.1) | collective-permute-done | bytes 262176 | tf_op jit(solution)/shard_map/ppermute | solution.py:21
  13.3 3.7 %collective-permute-start.3 = (f32[2,16,8,4]{3,2,1,0:T(8,128)S(1)}, f32[2,16,8,4]{3,2,1,0:T(8,128)S(1)}, u32[]{:S(2)}, u32[]{:S(2)}) collective-permute-start(f32[2,16,8,4]{3,2,1,0:T(8,128)S(1)} %get-tuple-element.14), channel_id=1, source_target_pairs={{2,0},{4,2},{6,4},{0,6},{3,1},{5,3},{7,5},{1,7},{10,8},{12,10},{14... | collective-permute-start | bytes 12296 | tf_op jit(solution)/shard_map/ppermute | solution.py:21
  17.0 3.9 %collective-permute-done.3 = f32[2,16,8,4]{3,2,1,0:T(8,128)S(1)} collective-permute-done((f32[2,16,8,4]{3,2,1,0:T(8,128)S(1)}, f32[2,16,8,4]{3,2,1,0:T(8,128)S(1)}, u32[]{:S(2)}, u32[]{:S(2)}) %collective-permute-start.3) | collective-permute-done | bytes 4128 | tf_op jit(solution)/shard_map/ppermute | solution.py:21
  20.9 3.8 %collective-permute-done.2 = f32[2,16,8,4]{3,2,1,0:T(8,128)S(1)} collective-permute-done((f32[2,16,8,4]{3,2,1,0:T(8,128)S(1)}, f32[2,16,8,4]{3,2,1,0:T(8,128)S(1)}, u32[]{:S(2)}, u32[]{:S(2)}) %collective-permute-start.2) | collective-permute-done | bytes 4128 | tf_op jit(solution)/shard_map/ppermute | solution.py:20
  25.5 5.1 %copy.97 = f32[2,16,8,1032]{1,2,3,0:T(8,128)} copy(f32[2,16,8,1032]{3,2,1,0:T(8,128)S(1)} %concatenate.56) | data formatting | bytes 2113536 | tf_op jit(solution)/shard_map/concatenate | solution.py:22
  30.6 7.3 %fusion.83 = (f32[2,16,8,516,1]{1,2,4,3,0:T(8,128)}, f32[2,16,8,516,1]{1,2,4,3,0:T(8,128)}) fusion(f32[2,16,8,516,2]{1,2,4,3,0:T(8,128)} %bitcast.55), kind=kLoop, calls=%fused_computation.166 | loop fusion | bytes 2113536 | tf_op jit(solution)/shard_map/slice | solution.py:35
  37.9 3.1 %copy.99 = f32[2,16,8,516,1]{3,2,1,0,4:T(8,128)S(1)} copy(f32[2,16,8,516,1]{1,2,4,3,0:T(8,128)} %get-tuple-element.4) | data formatting | bytes 1056768 | tf_op jit(solution)/shard_map/slice | solution.py:35
  41.0 3.1 %copy.115 = f32[2,16,8,516,1]{3,2,1,0,4:T(8,128)S(1)} copy(f32[2,16,8,516,1]{1,2,4,3,0:T(8,128)} %get-tuple-element.5) | data formatting | bytes 1056768
  45.6 1.6 %collective-permute-start.4 = (f32[4,4,8,512]{3,2,1,0:T(8,128)S(1)}, f32[4,4,8,512]{3,2,1,0:T(8,128)S(1)}, u32[]{:S(2)}, u32[]{:S(2)}) collective-permute-start(f32[4,4,8,512]{3,2,1,0:T(8,128)S(1)} %get-tuple-element.12), channel_id=1, source_target_pairs={{0,1},{1,0},{2,3},{3,2},{4,5},{5,4},{6,7},{7,6},{8,9},{9,8},{10,11... | collective-permute-start | bytes 786440 | tf_op jit(solution)/shard_map/ppermute | solution.py:20
  47.7 7.2 %collective-permute-done.4 = f32[4,4,8,512]{3,2,1,0:T(8,128)S(1)} collective-permute-done((f32[4,4,8,512]{3,2,1,0:T(8,128)S(1)}, f32[4,4,8,512]{3,2,1,0:T(8,128)S(1)}, u32[]{:S(2)}, u32[]{:S(2)}) %collective-permute-start.4) | collective-permute-done | bytes 262176 | tf_op jit(solution)/shard_map/ppermute | solution.py:20
  54.9 4.3 %collective-permute-done.5 = f32[4,4,8,512]{3,2,1,0:T(8,128)S(1)} collective-permute-done((f32[4,4,8,512]{3,2,1,0:T(8,128)S(1)}, f32[4,4,8,512]{3,2,1,0:T(8,128)S(1)}, u32[]{:S(2)}, u32[]{:S(2)}) %collective-permute-start.5) | collective-permute-done | bytes 262176 | tf_op jit(solution)/shard_map/ppermute | solution.py:21
  61.0 1.7 %collective-permute-start.7 = (f32[1,8,4,512]{3,2,1,0:T(4,128)S(1)}, f32[1,8,4,512]{3,2,1,0:T(4,128)S(1)}, u32[]{:S(2)}, u32[]{:S(2)}) collective-permute-start(f32[1,8,4,512]{3,2,1,0:T(4,128)S(1)} %get-tuple-element.27), channel_id=1, source_target_pairs={{8,0},{16,8},{24,16},{0,24},{9,1},{17,9},{25,17},{1,25},{10,2},{18... | collective-permute-start | bytes 196616 | tf_op jit(solution)/shard_map/ppermute | solution.py:21
  62.7 1.9 %collective-permute-done.6 = f32[1,8,4,512]{3,2,1,0:T(4,128)S(1)} collective-permute-done((f32[1,8,4,512]{3,2,1,0:T(4,128)S(1)}, f32[1,8,4,512]{3,2,1,0:T(4,128)S(1)}, u32[]{:S(2)}, u32[]{:S(2)}) %collective-permute-start.6) | collective-permute-done | bytes 65568 | tf_op jit(solution)/shard_map/ppermute | solution.py:20
  67.0 2.3 %collective-permute-start.9 = (f32[2,8,4,4]{3,1,2,0:T(8,128)S(1)}, f32[2,8,4,4]{3,1,2,0:T(8,128)S(1)}, u32[]{:S(2)}, u32[]{:S(2)}) collective-permute-start(f32[2,8,4,4]{3,1,2,0:T(8,128)S(1)} %get-tuple-element.35), channel_id=1, source_target_pairs={{2,0},{4,2},{6,4},{0,6},{3,1},{5,3},{7,5},{1,7},{10,8},{12,10},{14... | collective-permute-start | bytes 3080 | tf_op jit(solution)/shard_map/ppermute | solution.py:21
  69.3 2.0 %collective-permute-done.8 = f32[2,8,4,4]{3,1,2,0:T(8,128)S(1)} collective-permute-done((f32[2,8,4,4]{3,1,2,0:T(8,128)S(1)}, f32[2,8,4,4]{3,1,2,0:T(8,128)S(1)}, u32[]{:S(2)}, u32[]{:S(2)}) %collective-permute-start.8) | collective-permute-done | bytes 1056 | tf_op jit(solution)/shard_map/ppermute | solution.py:20
  72.2 2.7 %fusion.84 = (f32[2,8,4,260,1]{1,4,3,2,0:T(1,128)}, f32[2,8,4,260,1]{1,4,3,2,0:T(1,128)S(1)}) fusion(f32[2,8,4,260,2]{1,4,3,2,0:T(2,128)S(1)} %bitcast.58), kind=kLoop, calls=%fused_computation.167 | loop fusion | bytes 266240 | tf_op jit(solution)/shard_map/slice | solution.py:35
  74.9 2.3 %copy.105 = f32[2,8,4,260,1]{3,1,4,2,0:T(8,128)S(1)} copy(f32[2,8,4,260,1]{1,4,3,2,0:T(1,128)} %get-tuple-element.6) | data formatting | bytes 133120 | tf_op jit(solution)/shard_map/slice | solution.py:35
  78.3 1.6 %collective-permute-start.10 = (f32[4,4,4,256]{3,1,2,0:T(4,128)S(1)}, f32[4,4,4,256]{3,1,2,0:T(4,128)S(1)}, u32[]{:S(2)}, u32[]{:S(2)}) collective-permute-start(f32[4,4,4,256]{3,1,2,0:T(4,128)S(1)} %get-tuple-element.32), channel_id=1, source_target_pairs={{0,1},{1,0},{2,3},{3,2},{4,5},{5,4},{6,7},{7,6},{8,9},{9,8},{10,11... | collective-permute-start | bytes 196616 | tf_op jit(solution)/shard_map/ppermute | solution.py:20
  80.4 2.5 %collective-permute-done.10 = f32[4,4,4,256]{3,1,2,0:T(4,128)S(1)} collective-permute-done((f32[4,4,4,256]{3,1,2,0:T(4,128)S(1)}, f32[4,4,4,256]{3,1,2,0:T(4,128)S(1)}, u32[]{:S(2)}, u32[]{:S(2)}) %collective-permute-start.10) | collective-permute-done | bytes 65568 | tf_op jit(solution)/shard_map/ppermute | solution.py:20
  86.4 1.8 %collective-permute-done.12 = f32[1,4,4,256]{3,2,1,0:T(4,128)S(1)} collective-permute-done((f32[1,4,4,256]{3,2,1,0:T(4,128)S(1)}, f32[1,4,4,256]{3,2,1,0:T(4,128)S(1)}, u32[]{:S(2)}, u32[]{:S(2)}) %collective-permute-start.12) | collective-permute-done | bytes 16416 | tf_op jit(solution)/shard_map/ppermute | solution.py:20
  88.5 3.7 %collective-permute-start.15 = (f32[2,4,2,4]{3,1,2,0:T(4,128)S(1)}, f32[2,4,2,4]{3,1,2,0:T(4,128)S(1)}, u32[]{:S(2)}, u32[]{:S(2)}) collective-permute-start(f32[2,4,2,4]{3,1,2,0:T(4,128)S(1)} %get-tuple-element.49), channel_id=1, source_target_pairs={{2,0},{4,2},{6,4},{0,6},{3,1},{5,3},{7,5},{1,7},{10,8},{12,10},{14... | collective-permute-start | bytes 776 | tf_op jit(solution)/shard_map/ppermute | solution.py:21
  (102 shorter events, 24.6 us)
Async XLA Ops:
  2.5 6.7 %collective-permute-start = (f32[1,16,4,1024]{3,1,2,0:T(8,128)S(1)}, f32[1,16,4,1024]{3,1,2,0:T(8,128)S(1)}, u32[]{:S(2)}, u32[]{:S(2)}) collective-permute-start(f32[1,16,4,1024]{3,1,2,0:T(8,128)S(1)} %get-tuple-element.16), channel_id=1, source_target_pairs={{0,8},{8,16},{16,24},{24,0},{1,9},{9,17},{17,25},{25,1},{2,10},{10... | collective-permute-start | bytes 786440 | tf_op jit(solution)/shard_map/ppermute | solution.py:20
  3.0 8.6 %collective-permute-start.1 = (f32[1,16,4,1024]{3,1,2,0:T(8,128)S(1)}, f32[1,16,4,1024]{3,1,2,0:T(8,128)S(1)}, u32[]{:S(2)}, u32[]{:S(2)}) collective-permute-start(f32[1,16,4,1024]{3,1,2,0:T(8,128)S(1)} %get-tuple-element.17), channel_id=1, source_target_pairs={{8,0},{16,8},{24,16},{0,24},{9,1},{17,9},{25,17},{1,25},{10,2},{18... | collective-permute-start | bytes 786440 | tf_op jit(solution)/shard_map/ppermute | solution.py:21
  13.3 7.6 %collective-permute-start.3 = (f32[2,16,8,4]{3,2,1,0:T(8,128)S(1)}, f32[2,16,8,4]{3,2,1,0:T(8,128)S(1)}, u32[]{:S(2)}, u32[]{:S(2)}) collective-permute-start(f32[2,16,8,4]{3,2,1,0:T(8,128)S(1)} %get-tuple-element.14), channel_id=1, source_target_pairs={{2,0},{4,2},{6,4},{0,6},{3,1},{5,3},{7,5},{1,7},{10,8},{12,10},{14... | collective-permute-start | bytes 12296 | tf_op jit(solution)/shard_map/ppermute | solution.py:21
  17.0 7.7 %collective-permute-start.2 = (f32[2,16,8,4]{3,2,1,0:T(8,128)S(1)}, f32[2,16,8,4]{3,2,1,0:T(8,128)S(1)}, u32[]{:S(2)}, u32[]{:S(2)}) collective-permute-start(f32[2,16,8,4]{3,2,1,0:T(8,128)S(1)} %get-tuple-element.15), channel_id=1, source_target_pairs={{0,2},{2,4},{4,6},{6,0},{1,3},{3,5},{5,7},{7,1},{8,10},{10,12},{12... | collective-permute-start | bytes 12296 | tf_op jit(solution)/shard_map/ppermute | solution.py:20
  45.6 9.3 %collective-permute-start.4 = (f32[4,4,8,512]{3,2,1,0:T(8,128)S(1)}, f32[4,4,8,512]{3,2,1,0:T(8,128)S(1)}, u32[]{:S(2)}, u32[]{:S(2)}) collective-permute-start(f32[4,4,8,512]{3,2,1,0:T(8,128)S(1)} %get-tuple-element.12), channel_id=1, source_target_pairs={{0,1},{1,0},{2,3},{3,2},{4,5},{5,4},{6,7},{7,6},{8,9},{9,8},{10,11... | collective-permute-start | bytes 786440 | tf_op jit(solution)/shard_map/ppermute | solution.py:20
  47.1 12.1 %collective-permute-start.5 = (f32[4,4,8,512]{3,2,1,0:T(8,128)S(1)}, f32[4,4,8,512]{3,2,1,0:T(8,128)S(1)}, u32[]{:S(2)}, u32[]{:S(2)}) collective-permute-start(f32[4,4,8,512]{3,2,1,0:T(8,128)S(1)} %get-tuple-element.13), channel_id=1, source_target_pairs={{1,0},{0,1},{3,2},{2,3},{5,4},{4,5},{7,6},{6,7},{9,8},{8,9},{11,10... | collective-permute-start | bytes 786440 | tf_op jit(solution)/shard_map/ppermute | solution.py:21
  60.9 1.8 %copy-start = (f32[4,8,8,512]{3,2,1,0:T(8,128)}, f32[4,8,8,512]{3,2,1,0:T(8,128)S(1)}, u32[]{:S(2)}) copy-start(f32[4,8,8,512]{3,2,1,0:T(8,128)S(1)} %get-tuple-element.20) | copy-start | bytes 1572868
  60.9 3.7 %collective-permute-start.6 = (f32[1,8,4,512]{3,2,1,0:T(4,128)S(1)}, f32[1,8,4,512]{3,2,1,0:T(4,128)S(1)}, u32[]{:S(2)}, u32[]{:S(2)}) collective-permute-start(f32[1,8,4,512]{3,2,1,0:T(4,128)S(1)} %get-tuple-element.26), channel_id=1, source_target_pairs={{0,8},{8,16},{16,24},{24,0},{1,9},{9,17},{17,25},{25,1},{2,10},{10... | collective-permute-start | bytes 196616 | tf_op jit(solution)/shard_map/ppermute | solution.py:20
  61.0 3.7 %collective-permute-start.7 = (f32[1,8,4,512]{3,2,1,0:T(4,128)S(1)}, f32[1,8,4,512]{3,2,1,0:T(4,128)S(1)}, u32[]{:S(2)}, u32[]{:S(2)}) collective-permute-start(f32[1,8,4,512]{3,2,1,0:T(4,128)S(1)} %get-tuple-element.27), channel_id=1, source_target_pairs={{8,0},{16,8},{24,16},{0,24},{9,1},{17,9},{25,17},{1,25},{10,2},{18... | collective-permute-start | bytes 196616 | tf_op jit(solution)/shard_map/ppermute | solution.py:21
  65.4 5.9 %collective-permute-start.8 = (f32[2,8,4,4]{3,1,2,0:T(8,128)S(1)}, f32[2,8,4,4]{3,1,2,0:T(8,128)S(1)}, u32[]{:S(2)}, u32[]{:S(2)}) collective-permute-start(f32[2,8,4,4]{3,1,2,0:T(8,128)S(1)} %get-tuple-element.34), channel_id=1, source_target_pairs={{0,2},{2,4},{4,6},{6,0},{1,3},{3,5},{5,7},{7,1},{8,10},{10,12},{12... | collective-permute-start | bytes 3080 | tf_op jit(solution)/shard_map/ppermute | solution.py:20
  67.0 4.5 %collective-permute-start.9 = (f32[2,8,4,4]{3,1,2,0:T(8,128)S(1)}, f32[2,8,4,4]{3,1,2,0:T(8,128)S(1)}, u32[]{:S(2)}, u32[]{:S(2)}) collective-permute-start(f32[2,8,4,4]{3,1,2,0:T(8,128)S(1)} %get-tuple-element.35), channel_id=1, source_target_pairs={{2,0},{4,2},{6,4},{0,6},{3,1},{5,3},{7,5},{1,7},{10,8},{12,10},{14... | collective-permute-start | bytes 3080 | tf_op jit(solution)/shard_map/ppermute | solution.py:21
  78.3 4.6 %collective-permute-start.10 = (f32[4,4,4,256]{3,1,2,0:T(4,128)S(1)}, f32[4,4,4,256]{3,1,2,0:T(4,128)S(1)}, u32[]{:S(2)}, u32[]{:S(2)}) collective-permute-start(f32[4,4,4,256]{3,1,2,0:T(4,128)S(1)} %get-tuple-element.32), channel_id=1, source_target_pairs={{0,1},{1,0},{2,3},{3,2},{4,5},{5,4},{6,7},{7,6},{8,9},{9,8},{10,11... | collective-permute-start | bytes 196616 | tf_op jit(solution)/shard_map/ppermute | solution.py:20
  79.9 4.3 %collective-permute-start.11 = (f32[4,4,4,256]{3,1,2,0:T(4,128)S(1)}, f32[4,4,4,256]{3,1,2,0:T(4,128)S(1)}, u32[]{:S(2)}, u32[]{:S(2)}) collective-permute-start(f32[4,4,4,256]{3,1,2,0:T(4,128)S(1)} %get-tuple-element.33), channel_id=1, source_target_pairs={{1,0},{0,1},{3,2},{2,3},{5,4},{4,5},{7,6},{6,7},{9,8},{8,9},{11,10... | collective-permute-start | bytes 196616 | tf_op jit(solution)/shard_map/ppermute | solution.py:21
  84.2 8.0 %copy-start.1 = (f32[4,8,8,512]{3,2,1,0:T(8,128)S(1)}, f32[4,8,8,512]{3,2,1,0:T(8,128)}, u32[]{:S(2)}) copy-start(f32[4,8,8,512]{3,2,1,0:T(8,128)} %copy-done) | copy-start | bytes 1572868
  84.2 8.0 %copy-start.2 = (f32[4,8,8,512]{3,2,1,0:T(8,128)S(1)}, f32[4,8,8,512]{3,2,1,0:T(8,128)}, u32[]{:S(2)}) copy-start(f32[4,8,8,512]{3,2,1,0:T(8,128)} %get-tuple-element.21) | copy-start | bytes 1572868
  84.6 1.7 %collective-permute-start.13 = (f32[1,4,4,256]{3,2,1,0:T(4,128)S(1)}, f32[1,4,4,256]{3,2,1,0:T(4,128)S(1)}, u32[]{:S(2)}, u32[]{:S(2)}) collective-permute-start(f32[1,4,4,256]{3,2,1,0:T(4,128)S(1)} %slice.688), channel_id=1, source_target_pairs={{8,0},{16,8},{24,16},{0,24},{9,1},{17,9},{25,17},{1,25},{10,2},{18... | collective-permute-start | bytes 49160 | tf_op jit(solution)/shard_map/ppermute | solution.py:21
  84.9 3.2 %collective-permute-start.12 = (f32[1,4,4,256]{3,2,1,0:T(4,128)S(1)}, f32[1,4,4,256]{3,2,1,0:T(4,128)S(1)}, u32[]{:S(2)}, u32[]{:S(2)}) collective-permute-start(f32[1,4,4,256]{3,2,1,0:T(4,128)S(1)} %slice.688), channel_id=1, source_target_pairs={{0,8},{8,16},{16,24},{24,0},{1,9},{9,17},{17,25},{25,1},{2,10},{10... | collective-permute-start | bytes 49160 | tf_op jit(solution)/shard_map/ppermute | solution.py:20
  88.4 5.5 %collective-permute-start.14 = (f32[2,4,2,4]{3,1,2,0:T(4,128)S(1)}, f32[2,4,2,4]{3,1,2,0:T(4,128)S(1)}, u32[]{:S(2)}, u32[]{:S(2)}) collective-permute-start(f32[2,4,2,4]{3,1,2,0:T(4,128)S(1)} %get-tuple-element.48), channel_id=1, source_target_pairs={{0,2},{2,4},{4,6},{6,0},{1,3},{3,5},{5,7},{7,1},{8,10},{10,12},{12... | collective-permute-start | bytes 776 | tf_op jit(solution)/shard_map/ppermute | solution.py:20
  88.5 5.3 %collective-permute-start.15 = (f32[2,4,2,4]{3,1,2,0:T(4,128)S(1)}, f32[2,4,2,4]{3,1,2,0:T(4,128)S(1)}, u32[]{:S(2)}, u32[]{:S(2)}) collective-permute-start(f32[2,4,2,4]{3,1,2,0:T(4,128)S(1)} %get-tuple-element.49), channel_id=1, source_target_pairs={{2,0},{4,2},{6,4},{0,6},{3,1},{5,3},{7,5},{1,7},{10,8},{12,10},{14... | collective-permute-start | bytes 776 | tf_op jit(solution)/shard_map/ppermute | solution.py:21
  95.4 3.8 %collective-permute-start.17 = (f32[4,4,2,128]{3,2,1,0:T(2,128)S(1)}, f32[4,4,2,128]{3,2,1,0:T(2,128)S(1)}, u32[]{:S(2)}, u32[]{:S(2)}) collective-permute-start(f32[4,4,2,128]{3,2,1,0:T(2,128)S(1)} %pad_maximum_fusion.15), channel_id=1, source_target_pairs={{1,0},{0,1},{3,2},{2,3},{5,4},{4,5},{7,6},{6,7},{9,8},{8,9},{11,10... | collective-permute-start | bytes 49160 | tf_op jit(solution)/shard_map/ppermute | solution.py:21
  96.7 3.7 %collective-permute-start.16 = (f32[4,4,2,128]{3,2,1,0:T(2,128)S(1)}, f32[4,4,2,128]{3,2,1,0:T(2,128)S(1)}, u32[]{:S(2)}, u32[]{:S(2)}) collective-permute-start(f32[4,4,2,128]{3,2,1,0:T(2,128)S(1)} %pad_maximum_fusion.15), channel_id=1, source_target_pairs={{0,1},{1,0},{2,3},{3,2},{4,5},{5,4},{6,7},{7,6},{8,9},{9,8},{10,11... | collective-permute-start | bytes 49160 | tf_op jit(solution)/shard_map/ppermute | solution.py:20
where the time goes:
time: 102 us
  waiting for transfers between devices  39.5 us (39%)
  local copies, waits for them, and re-layouts  31 us (30%)
  starting transfers between devices  22.5 us (22%)
  other arithmetic  7.6 us (7%)
  between operations  1.16 us (1%)
    ppermute x9, waiting for transfers between devices, padded_2(): before = lax.ppermute(last, axis, up)  25.2 us
    slice x7, local copies, waits for them, and re-layouts, lift_padded(): odds = lax.index_in_dim(paired, 1, dim + 1, False)  16.3 us
    ppermute x9, starting transfers between devices, padded_2(): after = lax.ppermute(initial, axis, down)  16 us
    ppermute x9, waiting for transfers between devices, padded_2(): after = lax.ppermute(initial, axis, down)  14.3 us
    concatenate x6, local copies, waits for them, and re-layouts, padded_2(): x = jnp.concatenate([before, x, after], axis=dim)  6.99 us
    ppermute x9, starting transfers between devices, padded_2(): before = lax.ppermute(last, axis, up)  6.47 us
    unnamed x9, local copies, waits for them, and re-layouts  5.24 us
    concatenate x6, other arithmetic, lift_padded(): return jnp.concatenate([lower, upper], axis=0)  2.4 us
  transfers between devices with their start and end apart: 18, of which 16 were waited for; matrix products, arithmetic and copies ran while one was open for 2% of the time, Pallas kernels for 0%

commit v1 on v0

v1 whole, which is shorter than its diff:
```python
import functools

import jax
import jax.numpy as jnp
from jax import lax
from jax.experimental import pallas as pl
from jax.experimental.pallas import tpu as pltpu
from jax.sharding import PartitionSpec as P

ALPHA = -1.586134342
BETA = -0.05298011854
GAMMA = 0.8829110762
DELTA = 0.4435068522
ZETA = 1.149604398

MESH = pl.DeviceIdType.MESH
LANES = 128
HALO = 32
F32 = jnp.float32
BF16 = jnp.bfloat16


def boundary_states(get, n):
    s0, last_s = get(0), get(n - 2)
    lead = get(1) + ALPHA * (s0 + get(2))
    trail = get(n - 3) + ALPHA * (get(n - 4) + last_s)
    return s0, s0 + BETA * lead, get(n - 1) + ALPHA * last_s, last_s + BETA * trail


def lift(get, n, from_left, from_right):
    m = n // 2
    s = [get(2 * i) for i in range(m)]
    d = [get(2 * i + 1) for i in range(m)]
    r, q = from_left
    s_next, p = from_right
    d1 = [r + ALPHA * s[0]]
    for i in range(m):
        d1.append(d[i] + ALPHA * (s[i] + (s[i + 1] if i + 1 < m else s_next)))
    s1 = [q + BETA * d1[0]]
    for i in range(m):
        s1.append(s[i] + BETA * (d1[i] + d1[i + 1]))
    s1.append(p + BETA * d1[m])
    d2 = [d1[i] + GAMMA * (s1[i] + s1[i + 1]) for i in range(m + 1)]
    low = [s1[i + 1] + DELTA * (d2[i] + d2[i + 1]) for i in range(m)]
    return low, d2[1:]


def lift_lanes(even, odd):
    width = even.shape[-1]
    after = lambda v: pltpu.roll(v, width - 1, 1)
    before = lambda v: pltpu.roll(v, 1, 1)
    d = odd + ALPHA * (even + after(even))
    s = even + BETA * (before(d) + d)
    d = d + GAMMA * (s + after(s))
    s = s + DELTA * (before(d) + d)
    return s, d


def exact_select(x, choose):
    total = None
    for _ in range(3):
        part = x.astype(BF16)
        x = x - part.astype(F32)
        term = jnp.dot(part, choose, preferred_element_type=F32)
        total = term if total is None else total + term
    return total


def split_matrix(depth):
    k = lax.broadcasted_iota(jnp.int32, (depth, 2 * LANES), 0)
    n = lax.broadcasted_iota(jnp.int32, (depth, 2 * LANES), 1)
    parity = (n >= LANES).astype(jnp.int32)
    n = n - LANES * parity
    if depth == LANES:
        n = jnp.where(n < LANES // 2, n, n - LANES // 2)
    return (k == 2 * n + parity).astype(BF16)


class Level:
    def __init__(self, index, nz, nx, pairs, source, refs, sems, sem_base, peers, chunks):
        self.index, self.nz, self.nx, self.pairs = index, nz, nx, pairs
        self.source = source
        (self.split, self.zs_l, self.zs_r, self.zr_l, self.zr_r, self.xs_l, self.xs_r, self.xr_l, self.xr_r,
         self.cs, self.cr, self.own_x, self.halo_x, self.both, self.staged) = refs
        self.send_sems, self.recv_sems = sems
        self.peers = peers
        self.chunks = chunks
        self.sem_base = sem_base
        self.copies = [self.make_copies(c) for c in range(len(chunks))]

    def make_copies(self, c):
        start, stop = self.chunks[c]
        tiles = pl.ds(2 * start, 2 * (stop - start))
        p = self.peers
        moves = [
            (self.zs_l.at[tiles], self.zr_r.at[tiles], p["z"][0]),
            (self.zs_r.at[tiles], self.zr_l.at[tiles], p["z"][1]),
        ]
        for sx in (0, 1):
            for sz in (0, 1):
                moves.append((self.cs.at[sx, sz, tiles], self.cr.at[1 - sx, 1 - sz, tiles], p["xz"][sx][sz]))
        moves.append((self.xs_l.at[tiles], self.xr_r.at[tiles], p["x"][0]))
        moves.append((self.xs_r.at[tiles], self.xr_l.at[tiles], p["x"][1]))
        return [
            pltpu.make_async_remote_copy(
                src_ref=src, dst_ref=dst,
                send_sem=self.send_sems.at[self.sem_base + 8 * c + i],
                recv_sem=self.recv_sems.at[self.sem_base + 8 * c + i],
                device_id=where, device_id_type=MESH,
            )
            for i, (src, dst, where) in enumerate(moves)
        ]

    def split_pair(self, j):
        if isinstance(j, int) and j == self.pairs:
            x = self.source[2 * self.pairs]
            both = exact_select(x, split_matrix(LANES))
        else:
            x = jnp.concatenate([self.source[2 * j], self.source[2 * j + 1]], axis=1)
            both = exact_select(x, split_matrix(2 * LANES))
        self.split[2 * j] = both[:, :LANES]
        self.split[2 * j + 1] = both[:, LANES:]

    def tile_states(self, t):
        nz, nx = self.nz, self.nx
        states = boundary_states(lambda z: self.split[t, z * nx:(z + 1) * nx, :], nz)
        self.zs_l[t, 0:nx, :] = states[0]
        self.zs_l[t, nx:2 * nx, :] = states[1]
        self.zs_r[t, 0:nx, :] = states[2]
        self.zs_r[t, nx:2 * nx, :] = states[3]
        states = boundary_states(lambda x: self.split[t, pl.ds(x, nz, stride=nx), :], nx)
        self.xs_l[t, 0] = states[0]
        self.xs_l[t, 1] = states[1]
        self.xs_r[t, 0] = states[2]
        self.xs_r[t, 1] = states[3]
        for sz, ref in enumerate((self.zs_l, self.zs_r)):
            states = boundary_states(lambda x: ref[t, pl.ds(x, 2, stride=nx), :], nx)
            for i, state in enumerate(states):
                self.cs[i // 2, sz, t, i % 2] = state

    def prepare(self, c):
        start, stop = self.chunks[c]
        main = min(stop, self.pairs)
        if main - start > 1:
            pl.loop(start, main)(self.split_pair)
        else:
            for j in range(start, main):
                self.split_pair(j)
        if stop > self.pairs:
            self.split_pair(self.pairs)
        pl.loop(2 * start, 2 * stop)(self.tile_states)

    def send(self, c):
        for copy in self.copies[c]:
            copy.start()

    def tile_planes(self, t):
        nz, nx = self.nz, self.nx
        mx = nx // 2
        bands = lift(
            lambda x: self.split[t, pl.ds(x, nz, stride=nx), :], nx,
            (self.xr_l[t, 0], self.xr_l[t, 1]), (self.xr_r[t, 0], self.xr_r[t, 1]),
        )
        for band, lines in enumerate(bands):
            for i, line in enumerate(lines):
                self.own_x[band, t, pl.ds(i, nz, stride=mx), :] = line
        for sz, ref in enumerate((self.zr_l, self.zr_r)):
            bands = lift(
                lambda x: ref[t, pl.ds(x, 2, stride=nx), :], nx,
                (self.cr[0, sz, t, 0], self.cr[0, sz, t, 1]), (self.cr[1, sz, t, 0], self.cr[1, sz, t, 1]),
            )
            for band, lines in enumerate(bands):
                for i, line in enumerate(lines):
                    self.halo_x[band, sz, t, pl.ds(i, 2, stride=mx), :] = line
        for xb in (0, 1):
            bands = lift(
                lambda z: self.own_x[xb, t, z * mx:(z + 1) * mx, :], nz,
                (self.halo_x[xb, 0, t, 0:mx, :], self.halo_x[xb, 0, t, mx:2 * mx, :]),
                (self.halo_x[xb, 1, t, 0:mx, :], self.halo_x[xb, 1, t, mx:2 * mx, :]),
            )
            for zb, lines in enumerate(bands):
                for i, line in enumerate(lines):
                    self.both[2 * zb + xb, t, i * mx:(i + 1) * mx, :] = line

    def receive(self, c):
        for copy in self.copies[c]:
            copy.wait_recv()
        start, stop = self.chunks[c]
        pl.loop(2 * start, 2 * stop)(self.tile_planes)

    def lines(self, band, rows_from, planes, approx):
        zb, xb = band // 2, band % 2
        mx = self.nx // 2
        rows = pl.ds(rows_from * mx, planes * mx)
        even = jnp.concatenate([self.both[band, 2 * j, rows, :] for j in range(self.pairs + 1)], axis=1)
        odd = jnp.concatenate([self.both[band, 2 * j + 1, rows, :] for j in range(self.pairs + 1)], axis=1)
        low, high = lift_lanes(even, odd)
        width = self.pairs * LANES
        low = low * ZETA ** (3 - 2 * (zb + xb))
        high = high[:, :width] * ZETA ** (1 - 2 * (zb + xb))
        if band == 0:
            for j in range(self.pairs + 1):
                approx[j, rows, :] = low[:, j * LANES:(j + 1) * LANES]
        for i in range(planes):
            if band > 0:
                self.staged[4 * zb + xb - 1, rows_from + i] = low[i * mx:(i + 1) * mx, :width]
            self.staged[4 * zb + 2 + xb - 1, rows_from + i] = high[i * mx:(i + 1) * mx]

    def all_lines(self, bands, approx=None):
        planes = self.nz // 2
        step = min(planes, 2)
        for band in bands:
            if planes // step > 1:
                pl.loop(0, planes // step)(lambda k, band=band: self.lines(band, k * step, step, approx))
            else:
                self.lines(band, 0, step, approx)


def buffers(nz, nx, pairs):
    tiles = 2 * (pairs + 1)
    shapes = [(tiles, nz * nx, LANES)]
    shapes += [(tiles, 2 * nx, LANES)] * 4
    shapes += [(tiles, 2, nz, LANES)] * 4
    shapes += [(2, 2, tiles, 2, 2, LANES)] * 2
    shapes += [(2, tiles, nz * nx // 2, LANES), (2, 2, tiles, nx, LANES)]
    shapes += [(4, tiles, nz * nx // 4, LANES)]
    shapes += [(7, nz // 2, nx // 2, pairs * LANES)]
    return [pltpu.VMEM(shape, F32) for shape in shapes]


def kernel(sizes, axes, u_ref, one_ref, two_ref, three_ref, approx_ref, *scratch):
    scratch = list(scratch)
    send_sems, recv_sems, in_sems, out_sems, raw, pack_l, pack_r, halo_l, halo_r, approx_four, approx_five, last = scratch[:12]
    rest = scratch[12:]
    per_level = len(rest) // 3
    gx, gy, gz = axes
    ix, iy, iz = (lax.axis_index(a) for a in ("gx", "gy", "gz"))
    around = lambda i, n: (lax.rem(i + n - 1, n), lax.rem(i + 1, n))
    near_x, near_y, near_z = around(ix, gx), around(iy, gy), around(iz, gz)
    peers = {
        "x": [(x, iy, iz) for x in near_x],
        "y": [(ix, y, iz) for y in near_y],
        "z": [(ix, iy, z) for z in near_z],
        "xz": [[(x, iy, z) for z in near_z] for x in near_x],
    }
    (nz, nx, pairs) = sizes[0]
    tiles = 2 * pairs

    loads = [
        pltpu.make_async_copy(u_ref.at[:, :, pl.ds(t * LANES, LANES)], raw.at[t], in_sems.at[t])
        for t in range(tiles)
    ]
    order = [0, tiles - 1] + list(range(1, tiles - 1))
    for t in order:
        loads[t].start()

    barrier = pltpu.get_barrier_semaphore()
    greeted = peers["x"] + peers["y"] + peers["z"] + peers["xz"][0] + peers["xz"][1]
    for where in greeted:
        pl.semaphore_signal(barrier, inc=1, device_id=where, device_id_type=MESH)

    half = pairs // 2
    levels = []
    base = 2
    for index, (lz, lx, lp) in enumerate(sizes):
        chunks = [(0, half), (half, lp), (lp, lp + 1)] if index == 0 else [(0, lp + 1)]
        source = [raw.reshape(tiles + 1, nz * nx, LANES), approx_four, approx_five][index]
        levels.append(Level(index, lz, lx, lp, source, rest[index * per_level:(index + 1) * per_level],
                            (send_sems, recv_sems), base, peers, chunks))
        base += 8 * len(chunks)
    first, second, third = levels

    groups = LANES // HALO
    part = nz * nx // groups
    lane = lax.broadcasted_iota(jnp.int32, (part, LANES), 1)
    loads[0].wait()
    loads[tiles - 1].wait()
    flat = first.source

    def gather(tile, offset):
        total = None
        for g in range(groups):
            rows = pltpu.roll(flat[tile, g * part:(g + 1) * part, :], (g * HALO - offset) % LANES, 1)
            total = rows if total is None else jnp.where(lane >= g * HALO, rows, total)
        return total

    pack_l[...] = gather(0, 0)
    pack_r[...] = gather(tiles - 1, LANES - HALO)
    for t in range(1, tiles - 1):
        loads[t].wait()
    first.prepare(0)

    pl.semaphore_wait(barrier, len(greeted))
    y_copies = [
        pltpu.make_async_remote_copy(src_ref=src, dst_ref=dst, send_sem=send_sems.at[i], recv_sem=recv_sems.at[i],
                                     device_id=where, device_id_type=MESH)
        for i, (src, dst, where) in enumerate(((pack_l, halo_r, peers["y"][0]), (pack_r, halo_l, peers["y"][1])))
    ]
    for copy in y_copies:
        copy.start()
    first.send(0)
    first.prepare(1)
    first.send(1)
    for copy in y_copies:
        copy.wait_recv()
    for g in range(groups):
        after = pltpu.roll(halo_r[...], (-g * HALO) % LANES, 1)
        before = pltpu.roll(halo_l[...], (LANES - HALO - g * HALO) % LANES, 1)
        flat[tiles, g * part:(g + 1) * part, :] = jnp.where(
            lane < HALO, after, jnp.where(lane >= LANES - HALO, before, 0.0)
        )
    first.prepare(2)
    first.send(2)
    for c in range(3):
        first.receive(c)
    first.all_lines([0], approx_four)

    second.prepare(0)
    second.send(0)
    first.all_lines([1, 2, 3])
    store_one = pltpu.make_async_copy(first.staged, one_ref, out_sems.at[0])
    store_one.start()
    second.receive(0)
    second.all_lines([0], approx_five)

    third.prepare(0)
    third.send(0)
    second.all_lines([1, 2, 3])
    store_two = pltpu.make_async_copy(second.staged, two_ref, out_sems.at[1])
    store_two.start()
    third.receive(0)
    third.all_lines([0, 1, 2, 3], last)
    store_three = pltpu.make_async_copy(third.staged, three_ref, out_sems.at[2])
    store_three.start()
    mz, mx = third.nz // 2, third.nx // 2
    stores = [store_one, store_two, store_three]
    for i in range(mz):
        store = pltpu.make_async_copy(last.at[0, pl.ds(i * mx, mx)], approx_ref.at[i], out_sems.at[3 + i])
        store.start()
        stores.append(store)

    for copy in y_copies:
        copy.wait_send()
    for level in levels:
        for copies in level.copies:
            for copy in copies:
                copy.wait_send()
    for store in stores:
        store.wait()


def solution(mesh):
    axes = tuple(mesh.shape[a] for a in ("gx", "gy", "gz"))

    def on_device(density):
        nz, nx, ny = density.shape
        sizes = [(nz >> i, nx >> i, (ny >> i) // (2 * LANES)) for i in range(3)]
        tiles = ny // LANES
        shapes = [(7, z // 2, x // 2, p * LANES) for z, x, p in sizes]
        shapes.append(shapes[-1][1:])
        n_sems = 2 + 8 * 5
        packed = (nz * nx * HALO // LANES, LANES)
        scratch = [
            pltpu.SemaphoreType.DMA((n_sems,)),
            pltpu.SemaphoreType.DMA((n_sems,)),
            pltpu.SemaphoreType.DMA((tiles,)),
            pltpu.SemaphoreType.DMA((3 + shapes[-1][0],)),
            pltpu.VMEM((tiles + 1, nz, nx, LANES), F32),
        ]
        scratch += [pltpu.VMEM(packed, F32)] * 4
        for z, x, p in sizes:
            scratch.append(pltpu.VMEM((p + 1, z * x // 4, LANES), F32))
        for z, x, p in sizes:
            scratch += buffers(z, x, p)
        return pl.pallas_call(
            functools.partial(kernel, sizes, axes),
            out_shape=[jax.ShapeDtypeStruct(shape, F32) for shape in shapes],
            in_specs=[pl.BlockSpec(memory_space=pl.ANY)],
            out_specs=[pl.BlockSpec(memory_space=pl.ANY)] * 4,
            scratch_shapes=scratch,
            compiler_params=pltpu.CompilerParams(
                collective_id=0, has_side_effects=True, vmem_limit_bytes=40 << 20
            ),
            cost_estimate=pl.CostEstimate(flops=20_000_000, bytes_accessed=2 << 20, transcendentals=0),
        )(density)

    return jax.shard_map(
        on_device,
        mesh=mesh,
        in_specs=(P("gz", "gx", "gy"),),
        out_specs=(
            P(None, "gz", "gx", "gy"),
            P(None, "gz", "gx", "gy"),
            P(None, "gz", "gx", "gy"),
            P("gz", "gx", "gy"),
        ),
        check_vma=False,
    )
```

time: 102 us -> 34.4 us (0.34)
  waiting for transfers between devices: 39.5 us -> 0 us
  Pallas kernels: 0 us -> 29.4 us
  local copies, waits for them, and re-layouts: 31 us -> 3.97 us
  starting transfers between devices: 22.5 us -> 0 us
  other arithmetic: 7.6 us -> 0 us
    ppermute x18 -> x0, waiting for transfers between devices: 39.5 us -> none  [the longest x9 25.2 us: padded_2(): before = lax.ppermute(last, axis, up)]
    pallas_call x0 -> x1, Pallas kernels: none -> 29.4 us  [on_device(): pl.pallas_call(functools.partial(kernel, sizes, axes), out_shape=[jax.Sha...]
    ppermute x18 -> x0, starting transfers between devices: 22.5 us -> none  [the longest x9 16 us: padded_2(): after = lax.ppermute(initial, axis, down)]
    slice x14 -> x0, local copies, waits for them, and re-layouts: 17.3 us -> none  [the longest x7 16.3 us: lift_padded(): odds = lax.index_in_dim(paired, 1, dim + 1, False)]
    concatenate x7 -> x0, local copies, waits for them, and re-layouts: 7.3 us -> none  [the longest x6 6.99 us: padded_2(): x = jnp.concatenate([before, x, after], axis=dim)]
    concatenate x14 -> x0, other arithmetic: 3.01 us -> none  [the longest x6 2.4 us: lift_padded(): return jnp.concatenate([lower, upper], axis=0)]
    add x27 -> x0, other arithmetic: 2.71 us -> none  [the longest x9 0.96 us: lift_padded(): cut(evens, 1, half + 3, dim)]
    mul x8 -> x0, other arithmetic: 1.59 us -> none  [lift_padded(): lower = second_s * ZETA]
  transfers between devices with their start and end apart: 18 -> 0, of which waited for: 16 -> 0; matrix products, arithmetic and copies ran while one was open for 2% -> 0% of each run, Pallas kernels for 0% -> 0%
where the time goes in v1:
time: 34.4 us; the launch traced here: 34 us
  Pallas kernels  29.4 us (85%)
  local copies, waits for them, and re-layouts  3.97 us (12%)
  between operations  0.65 us (2%)
    pallas_call x1, Pallas kernels, on_device(): pl.pallas_call(functools.partial(kernel, sizes, axes), out_shape=[jax.Sha...  29.4 us
    unnamed x6, local copies, waits for them, and re-layouts  3.97 us

profile of v1, /device:TPU:0, one launch (start us, length us, event | category | flops | bytes accessed | tf_op | source)
XLA Modules:
  0.0 34.0 jit_solution(4413688947587380003)
XLA Ops:
  0.6 0.0 copy-start
  0.6 1.2 %copy-done = f32[16,16,1024]{2,1,0:T(8,128)S(1)} copy-done((f32[16,16,1024]{2,1,0:T(8,128)S(1)}, f32[16,16,1024]{2,1,0:T(8,128)}, u32[]{:S(2)}) %copy-start) | copy-done | bytes 1048600
  1.9 29.4 %shard_map.46 = (f32[7,8,8,512]{3,2,1,0:T(8,128)S(1)}, f32[7,4,4,256]{3,2,1,0:T(4,128)S(1)}, f32[7,2,2,128]{3,2,1,0:T(2,128)S(1)}, f32[2,2,128]{2,1,0:T(2,128)S(1)}) custom-call(f32[16,16,1024]{2,1,0:T(8,128)S(1)} %copy-done), custom_call_target="tpu_custom_call" | custom-call | flops 20000000 | bytes 2097152 | tf_op jit(solution)/shard_map/pallas_call | solution.py:375
  31.3 0.9 %copy.9 = f32[7,8,8,512]{3,2,1,0:T(8,128)} copy(f32[7,8,8,512]{3,2,1,0:T(8,128)S(1)} %get-tuple-element.8) | data formatting | bytes 1835008
  32.2 0.6 %copy.10 = f32[7,4,4,256]{3,2,1,0:T(4,128)} copy(f32[7,4,4,256]{3,2,1,0:T(4,128)S(1)} %get-tuple-element.9) | data formatting | bytes 229376
  32.8 0.6 %copy.11 = f32[7,2,2,128]{3,2,1,0:T(2,128)} copy(f32[7,2,2,128]{3,2,1,0:T(2,128)S(1)} %get-tuple-element.10) | data formatting | bytes 28672
  33.4 0.6 %copy.12 = f32[2,2,128]{2,1,0:T(2,128)} copy(f32[2,2,128]{2,1,0:T(2,128)S(1)} %get-tuple-element.11) | data formatting | bytes 4096
Async XLA Ops:
  0.6 1.2 %copy-start = (f32[16,16,1024]{2,1,0:T(8,128)S(1)}, f32[16,16,1024]{2,1,0:T(8,128)}, u32[]{:S(2)}) copy-start(f32[16,16,1024]{2,1,0:T(8,128)} %u_ref.1) | copy-start | bytes 3145732

commit v2 on v1

--- a/solution.py
+++ b/solution.py
@@ -57,50 +57,52 @@
 
 
 def exact_select(x, choose):
-    total = None
+    parts = []
     for _ in range(3):
-        part = x.astype(BF16)
-        x = x - part.astype(F32)
-        term = jnp.dot(part, choose, preferred_element_type=F32)
-        total = term if total is None else total + term
-    return total
+        parts.append(x.astype(BF16))
+        x = x - parts[-1].astype(F32)
+    terms = jnp.dot(jnp.concatenate(parts, axis=0), choose, preferred_element_type=F32)
+    n = x.shape[0]
+    return terms[:n] + terms[n:2 * n] + terms[2 * n:]
 
 
 def split_matrix(depth):
-    k = lax.broadcasted_iota(jnp.int32, (depth, 2 * LANES), 0)
-    n = lax.broadcasted_iota(jnp.int32, (depth, 2 * LANES), 1)
-    parity = (n >= LANES).astype(jnp.int32)
-    n = n - LANES * parity
-    if depth == LANES:
-        n = jnp.where(n < LANES // 2, n, n - LANES // 2)
-    return (k == 2 * n + parity).astype(BF16)
+    k = lax.broadcasted_iota(jnp.int32, (depth, depth), 0)
+    n = lax.broadcasted_iota(jnp.int32, (depth, depth), 1)
+    return (k == jnp.where(n < depth // 2, 2 * n, 2 * n - depth + 1)).astype(BF16)
 
 
 class Level:
     def __init__(self, index, nz, nx, pairs, source, refs, sems, sem_base, peers, chunks):
         self.index, self.nz, self.nx, self.pairs = index, nz, nx, pairs
         self.source = source
-        (self.split, self.zs_l, self.zs_r, self.zr_l, self.zr_r, self.xs_l, self.xs_r, self.xr_l, self.xr_r,
-         self.cs, self.cr, self.own_x, self.halo_x, self.both, self.staged) = refs
+        (self.split, self.zs, self.zr, self.xs, self.xr, self.cs, self.cr,
+         self.own_x, self.halo_x, self.both, self.staged) = refs
         self.send_sems, self.recv_sems = sems
         self.peers = peers
         self.chunks = chunks
         self.sem_base = sem_base
         self.copies = [self.make_copies(c) for c in range(len(chunks))]
 
+    def tile_range(self, c):
+        start, stop = self.chunks[c]
+        return 2 * start, min(2 * stop, 2 * self.pairs + 1)
+
     def make_copies(self, c):
-        start, stop = self.chunks[c]
-        tiles = pl.ds(2 * start, 2 * (stop - start))
+        start, stop = self.tile_range(c)
+        tiles = pl.ds(start, stop - start)
         p = self.peers
+        side = 2 * self.nx
         moves = [
-            (self.zs_l.at[tiles], self.zr_r.at[tiles], p["z"][0]),
-            (self.zs_r.at[tiles], self.zr_l.at[tiles], p["z"][1]),
+            (self.zs.at[tiles, pl.ds(sz * side, side)], self.zr.at[tiles, pl.ds((1 - sz) * side, side)], p["z"][sz])
+            for sz in (0, 1)
         ]
         for sx in (0, 1):
             for sz in (0, 1):
-                moves.append((self.cs.at[sx, sz, tiles], self.cr.at[1 - sx, 1 - sz, tiles], p["xz"][sx][sz]))
-        moves.append((self.xs_l.at[tiles], self.xr_r.at[tiles], p["x"][0]))
-        moves.append((self.xs_r.at[tiles], self.xr_l.at[tiles], p["x"][1]))
+                moves.append((self.cs.at[sx, tiles, :, pl.ds(2 * sz, 2)],
+                              self.cr.at[1 - sx, tiles, :, pl.ds(2 - 2 * sz, 2)], p["xz"][sx][sz]))
+        for sx in (0, 1):
+            moves.append((self.xs.at[sx, tiles], self.xr.at[1 - sx, tiles], p["x"][sx]))
         return [
             pltpu.make_async_remote_copy(
                 src_ref=src, dst_ref=dst,
@@ -111,44 +113,42 @@
             for i, (src, dst, where) in enumerate(moves)
         ]
 
-    def split_pair(self, j):
-        if isinstance(j, int) and j == self.pairs:
-            x = self.source[2 * self.pairs]
-            both = exact_select(x, split_matrix(LANES))
-        else:
-            x = jnp.concatenate([self.source[2 * j], self.source[2 * j + 1]], axis=1)
-            both = exact_select(x, split_matrix(2 * LANES))
-        self.split[2 * j] = both[:, :LANES]
-        self.split[2 * j + 1] = both[:, LANES:]
+    def split_chunk(self, c):
+        start, stop = self.chunks[c]
+        main = min(stop, self.pairs)
+        rows = self.nz * self.nx
+        if start == self.pairs:
+            self.split[2 * start] = exact_select(self.source[2 * start], split_matrix(LANES))
+            return
+        firsts = [self.source[2 * j] for j in range(start, stop)]
+        seconds = [self.source[2 * j + 1 if j < main else 2 * j] for j in range(start, stop)]
+        x = jnp.concatenate([jnp.concatenate(firsts, axis=0), jnp.concatenate(seconds, axis=0)], axis=1)
+        both = exact_select(x, split_matrix(2 * LANES))
+        for i, j in enumerate(range(start, stop)):
+            even = both[i * rows:(i + 1) * rows, :LANES]
+            odd = both[i * rows:(i + 1) * rows, LANES:]
+            if j < main:
+                self.split[2 * j] = even
+                self.split[2 * j + 1] = odd
+            else:
+                lane = lax.broadcasted_iota(jnp.int32, (rows, LANES), 1)
+                self.split[2 * j] = jnp.where(lane < LANES // 2, even, odd)
 
     def tile_states(self, t):
         nz, nx = self.nz, self.nx
         states = boundary_states(lambda z: self.split[t, z * nx:(z + 1) * nx, :], nz)
-        self.zs_l[t, 0:nx, :] = states[0]
-        self.zs_l[t, nx:2 * nx, :] = states[1]
-        self.zs_r[t, 0:nx, :] = states[2]
-        self.zs_r[t, nx:2 * nx, :] = states[3]
+        for i, state in enumerate(states):
+            self.zs[t, i * nx:(i + 1) * nx, :] = state
         states = boundary_states(lambda x: self.split[t, pl.ds(x, nz, stride=nx), :], nx)
-        self.xs_l[t, 0] = states[0]
-        self.xs_l[t, 1] = states[1]
-        self.xs_r[t, 0] = states[2]
-        self.xs_r[t, 1] = states[3]
-        for sz, ref in enumerate((self.zs_l, self.zs_r)):
-            states = boundary_states(lambda x: ref[t, pl.ds(x, 2, stride=nx), :], nx)
-            for i, state in enumerate(states):
-                self.cs[i // 2, sz, t, i % 2] = state
+        for i, state in enumerate(states):
+            self.xs[i // 2, t, i % 2] = state
+        states = boundary_states(lambda x: self.zs[t, pl.ds(x, 4, stride=nx), :], nx)
+        for i, state in enumerate(states):
+            self.cs[i // 2, t, i % 2] = state
 
     def prepare(self, c):
-        start, stop = self.chunks[c]
-        main = min(stop, self.pairs)
-        if main - start > 1:
-            pl.loop(start, main)(self.split_pair)
-        else:
-            for j in range(start, main):
-                self.split_pair(j)
-        if stop > self.pairs:
-            self.split_pair(self.pairs)
-        pl.loop(2 * start, 2 * stop)(self.tile_states)
+        self.split_chunk(c)
+        pl.loop(*self.tile_range(c))(self.tile_states)
 
     def send(self, c):
         for copy in self.copies[c]:
@@ -159,25 +159,21 @@
         mx = nx // 2
         bands = lift(
             lambda x: self.split[t, pl.ds(x, nz, stride=nx), :], nx,
-            (self.xr_l[t, 0], self.xr_l[t, 1]), (self.xr_r[t, 0], self.xr_r[t, 1]),
+            (self.xr[0, t, 0], self.xr[0, t, 1]), (self.xr[1, t, 0], self.xr[1, t, 1]),
         )
         for band, lines in enumerate(bands):
             for i, line in enumerate(lines):
                 self.own_x[band, t, pl.ds(i, nz, stride=mx), :] = line
-        for sz, ref in enumerate((self.zr_l, self.zr_r)):
-            bands = lift(
-                lambda x: ref[t, pl.ds(x, 2, stride=nx), :], nx,
-                (self.cr[0, sz, t, 0], self.cr[0, sz, t, 1]), (self.cr[1, sz, t, 0], self.cr[1, sz, t, 1]),
-            )
-            for band, lines in enumerate(bands):
-                for i, line in enumerate(lines):
-                    self.halo_x[band, sz, t, pl.ds(i, 2, stride=mx), :] = line
+        bands = lift(
+            lambda x: self.zr[t, pl.ds(x, 4, stride=nx), :], nx,
+            (self.cr[0, t, 0], self.cr[0, t, 1]), (self.cr[1, t, 0], self.cr[1, t, 1]),
+        )
+        for band, lines in enumerate(bands):
+            for i, line in enumerate(lines):
+                self.halo_x[band, t, pl.ds(i, 4, stride=mx), :] = line
         for xb in (0, 1):
-            bands = lift(
-                lambda z: self.own_x[xb, t, z * mx:(z + 1) * mx, :], nz,
-                (self.halo_x[xb, 0, t, 0:mx, :], self.halo_x[xb, 0, t, mx:2 * mx, :]),
-                (self.halo_x[xb, 1, t, 0:mx, :], self.halo_x[xb, 1, t, mx:2 * mx, :]),
-            )
+            halo = [self.halo_x[xb, t, i * mx:(i + 1) * mx, :] for i in range(4)]
+            bands = lift(lambda z: self.own_x[xb, t, z * mx:(z + 1) * mx, :], nz, halo[:2], halo[2:])
             for zb, lines in enumerate(bands):
                 for i, line in enumerate(lines):
                     self.both[2 * zb + xb, t, i * mx:(i + 1) * mx, :] = line
@@ -185,15 +181,19 @@
     def receive(self, c):
         for copy in self.copies[c]:
             copy.wait_recv()
-        start, stop = self.chunks[c]
-        pl.loop(2 * start, 2 * stop)(self.tile_planes)
+        pl.loop(*self.tile_range(c))(self.tile_planes)
 
     def lines(self, band, rows_from, planes, approx):
         zb, xb = band // 2, band % 2
         mx = self.nx // 2
         rows = pl.ds(rows_from * mx, planes * mx)
-        even = jnp.concatenate([self.both[band, 2 * j, rows, :] for j in range(self.pairs + 1)], axis=1)
-        odd = jnp.concatenate([self.both[band, 2 * j + 1, rows, :] for j in range(self.pairs + 1)], axis=1)
+        ends = self.both[band, 2 * self.pairs, rows, :]
+        turned = pltpu.roll(ends, LANES // 2, 1)
+        near = lax.broadcasted_iota(jnp.int32, ends.shape, 1) < LANES // 2
+        evens = [self.both[band, 2 * j, rows, :] for j in range(self.pairs)]
+        odds = [self.both[band, 2 * j + 1, rows, :] for j in range(self.pairs)]
+        even = jnp.concatenate(evens + [jnp.where(near, ends, turned)], axis=1)
+        odd = jnp.concatenate(odds + [jnp.where(near, turned, ends)], axis=1)
         low, high = lift_lanes(even, odd)
         width = self.pairs * LANES
         low = low * ZETA ** (3 - 2 * (zb + xb))
@@ -217,15 +217,25 @@
 
 
 def buffers(nz, nx, pairs):
-    tiles = 2 * (pairs + 1)
+    tiles = 2 * pairs + 1
     shapes = [(tiles, nz * nx, LANES)]
-    shapes += [(tiles, 2 * nx, LANES)] * 4
-    shapes += [(tiles, 2, nz, LANES)] * 4
-    shapes += [(2, 2, tiles, 2, 2, LANES)] * 2
-    shapes += [(2, tiles, nz * nx // 2, LANES), (2, 2, tiles, nx, LANES)]
+    shapes += [(tiles, 4 * nx, LANES)] * 2
+    shapes += [(2, tiles, 2, nz, LANES)] * 2
+    shapes += [(2, tiles, 2, 4, LANES)] * 2
+    shapes += [(2, tiles, nz * nx // 2, LANES), (2, tiles, 2 * nx, LANES)]
     shapes += [(4, tiles, nz * nx // 4, LANES)]
     shapes += [(7, nz // 2, nx // 2, pairs * LANES)]
     return [pltpu.VMEM(shape, F32) for shape in shapes]
+
+
+def hand_out(*refs):
+    sems = refs[-1]
+    n = (len(refs) - 1) // 2
+    copies = [pltpu.make_async_copy(refs[i], refs[n + i], sems.at[i]) for i in range(n)]
+    for copy in copies:
+        copy.start()
+    for copy in copies:
+        copy.wait()
 
 
 def kernel(sizes, axes, u_ref, one_ref, two_ref, three_ref, approx_ref, *scratch):
@@ -372,10 +382,11 @@
             scratch.append(pltpu.VMEM((p + 1, z * x // 4, LANES), F32))
         for z, x, p in sizes:
             scratch += buffers(z, x, p)
-        return pl.pallas_call(
+        outs = [jax.ShapeDtypeStruct(shape, F32) for shape in shapes]
+        results = pl.pallas_call(
             functools.partial(kernel, sizes, axes),
-            out_shape=[jax.ShapeDtypeStruct(shape, F32) for shape in shapes],
-            in_specs=[pl.BlockSpec(memory_space=pl.ANY)],
+            out_shape=outs,
+            in_specs=[pl.BlockSpec(memory_space=pltpu.HBM)],
             out_specs=[pl.BlockSpec(memory_space=pl.ANY)] * 4,
             scratch_shapes=scratch,
             compiler_params=pltpu.CompilerParams(
@@ -383,6 +394,14 @@
             ),
             cost_estimate=pl.CostEstimate(flops=20_000_000, bytes_accessed=2 << 20, transcendentals=0),
         )(density)
+        return pl.pallas_call(
+            hand_out,
+            out_shape=outs,
+            in_specs=[pl.BlockSpec(memory_space=pl.ANY)] * 4,
+            out_specs=[pl.BlockSpec(memory_space=pltpu.HBM)] * 4,
+            scratch_shapes=[pltpu.SemaphoreType.DMA((4,))],
+            cost_estimate=pl.CostEstimate(flops=0, bytes_accessed=2 << 20, transcendentals=0),
+        )(*results)
 
     return jax.shard_map(
         on_device,

time: 34.4 us -> 65.6 us (1.91)
  Pallas kernels: 29.4 us -> 60.5 us
    pallas_call x1 -> x2, Pallas kernels: 29.4 us -> 60.5 us  [the longest x1 32.9 us: on_device(): pl.pallas_call(hand_out, out_shape=outs, in_specs=[pl.BlockSpec(memory_sp...]
    unnamed x6 -> x10, local copies, waits for them, and re-layouts: 3.97 us -> 3.97 us
where the time goes in v2:
time: 65.6 us; the launch traced here: 65.2 us
  Pallas kernels  60.5 us (92%)
  local copies, waits for them, and re-layouts  3.97 us (6%)
  between operations  0.66 us (1%)
    pallas_call x1, Pallas kernels, on_device(): pl.pallas_call(hand_out, out_shape=outs, in_specs=[pl.BlockSpec(memory_sp...  32.9 us
    pallas_call x1, Pallas kernels, on_device(): pl.pallas_call(functools.partial(kernel, sizes, axes), out_shape=outs, in...  27.6 us
    unnamed x10, local copies, waits for them, and re-layouts  3.97 us

profile of v2, /device:TPU:0, one launch (start us, length us, event | category | flops | bytes accessed | tf_op | source)
XLA Modules:
  0.0 65.2 jit_solution(510445513043308608)
XLA Ops:
  0.6 0.0 copy-start
  0.6 1.2 %copy-done = f32[16,16,1024]{2,1,0:T(8,128)S(1)} copy-done((f32[16,16,1024]{2,1,0:T(8,128)S(1)}, f32[16,16,1024]{2,1,0:T(8,128)}, u32[]{:S(2)}) %copy-start) | copy-done | bytes 1048600
  1.9 27.6 %shard_map.46 = (f32[7,8,8,512]{3,2,1,0:T(8,128)S(1)}, f32[7,4,4,256]{3,2,1,0:T(4,128)S(1)}, f32[7,2,2,128]{3,2,1,0:T(2,128)S(1)}, f32[2,2,128]{2,1,0:T(2,128)S(1)}) custom-call(f32[16,16,1024]{2,1,0:T(8,128)S(1)} %copy-done), custom_call_target="tpu_custom_call" | custom-call | flops 20000000 | bytes 2097152 | tf_op jit(solution)/shard_map/pallas_call | solution.py:386
  29.5 0.0 copy-start.1
  29.5 0.9 %copy-done.1 = f32[7,8,8,512]{3,2,1,0:T(8,128)} copy-done((f32[7,8,8,512]{3,2,1,0:T(8,128)}, f32[7,8,8,512]{3,2,1,0:T(8,128)S(1)}, u32[]{:S(2)}) %copy-start.1) | copy-done | bytes 917528
  30.4 0.0 copy-start.2
  30.4 0.7 %copy-done.2 = f32[7,4,4,256]{3,2,1,0:T(4,128)} copy-done((f32[7,4,4,256]{3,2,1,0:T(4,128)}, f32[7,4,4,256]{3,2,1,0:T(4,128)S(1)}, u32[]{:S(2)}) %copy-start.2) | copy-done | bytes 114712
  31.1 0.0 copy-start.3
  31.1 0.6 copy-done.3
  31.7 0.0 copy-start.4
  31.7 0.6 copy-done.4
  32.3 32.9 %shard_map.47 = (f32[7,8,8,512]{3,2,1,0:T(8,128)}, f32[7,4,4,256]{3,2,1,0:T(4,128)}, f32[7,2,2,128]{3,2,1,0:T(2,128)}, f32[2,2,128]{2,1,0:T(2,128)}) custom-call(f32[7,8,8,512]{3,2,1,0:T(8,128)} %copy-done.1, f32[7,4,4,256]{3,2,1,0:T(4,128)} %copy-done.2, f32[7,2,2,128]{3,2,1,0:T(2,128)} %copy-done.3, f32[2,2,128]{2,1,0:T(2,128)} %copy-done.4), custom_call_target="tpu_custom_call" | custom-call | bytes 2097152 | tf_op jit(solution)/shard_map/pallas_call | solution.py:397
Async XLA Ops:
  0.6 1.2 %copy-start = (f32[16,16,1024]{2,1,0:T(8,128)S(1)}, f32[16,16,1024]{2,1,0:T(8,128)}, u32[]{:S(2)}) copy-start(f32[16,16,1024]{2,1,0:T(8,128)} %u_ref.1) | copy-start | bytes 3145732
  29.5 0.9 %copy-start.1 = (f32[7,8,8,512]{3,2,1,0:T(8,128)}, f32[7,8,8,512]{3,2,1,0:T(8,128)S(1)}, u32[]{:S(2)}) copy-start(f32[7,8,8,512]{3,2,1,0:T(8,128)S(1)} %get-tuple-element.8.refs_0_) | copy-start | bytes 2752516
  30.4 0.7 %copy-start.2 = (f32[7,4,4,256]{3,2,1,0:T(4,128)}, f32[7,4,4,256]{3,2,1,0:T(4,128)S(1)}, u32[]{:S(2)}) copy-start(f32[7,4,4,256]{3,2,1,0:T(4,128)S(1)} %get-tuple-element.9.refs_1_) | copy-start | bytes 344068
  31.1 0.6 copy-start.3
  31.7 0.6 copy-start.4

commit v3 on v2

--- a/solution.py
+++ b/solution.py
@@ -73,11 +73,12 @@
 
 
 class Level:
-    def __init__(self, index, nz, nx, pairs, source, refs, sems, sem_base, peers, chunks):
+    def __init__(self, index, nz, nx, pairs, source, refs, details, sems, sem_base, peers, chunks):
         self.index, self.nz, self.nx, self.pairs = index, nz, nx, pairs
         self.source = source
         (self.split, self.zs, self.zr, self.xs, self.xr, self.cs, self.cr,
-         self.own_x, self.halo_x, self.both, self.staged) = refs
+         self.own_x, self.halo_x, self.both) = refs
+        self.details = details
         self.send_sems, self.recv_sems = sems
         self.peers = peers
         self.chunks = chunks
@@ -198,13 +199,15 @@
         width = self.pairs * LANES
         low = low * ZETA ** (3 - 2 * (zb + xb))
         high = high[:, :width] * ZETA ** (1 - 2 * (zb + xb))
-        if band == 0:
+        if band == 0 and self.index < 2:
             for j in range(self.pairs + 1):
                 approx[j, rows, :] = low[:, j * LANES:(j + 1) * LANES]
         for i in range(planes):
+            if band == 0 and self.index == 2:
+                approx[rows_from + i] = low[i * mx:(i + 1) * mx, :width]
             if band > 0:
-                self.staged[4 * zb + xb - 1, rows_from + i] = low[i * mx:(i + 1) * mx, :width]
-            self.staged[4 * zb + 2 + xb - 1, rows_from + i] = high[i * mx:(i + 1) * mx]
+                self.details[4 * zb + xb - 1, rows_from + i] = low[i * mx:(i + 1) * mx, :width]
+            self.details[4 * zb + 2 + xb - 1, rows_from + i] = high[i * mx:(i + 1) * mx]
 
     def all_lines(self, bands, approx=None):
         planes = self.nz // 2
@@ -224,7 +227,6 @@
     shapes += [(2, tiles, 2, 4, LANES)] * 2
     shapes += [(2, tiles, nz * nx // 2, LANES), (2, tiles, 2 * nx, LANES)]
     shapes += [(4, tiles, nz * nx // 4, LANES)]
-    shapes += [(7, nz // 2, nx // 2, pairs * LANES)]
     return [pltpu.VMEM(shape, F32) for shape in shapes]
 
 
@@ -240,8 +242,8 @@
 
 def kernel(sizes, axes, u_ref, one_ref, two_ref, three_ref, approx_ref, *scratch):
     scratch = list(scratch)
-    send_sems, recv_sems, in_sems, out_sems, raw, pack_l, pack_r, halo_l, halo_r, approx_four, approx_five, last = scratch[:12]
-    rest = scratch[12:]
+    send_sems, recv_sems, in_sems, raw, pack_l, pack_r, halo_l, halo_r, approx_four, approx_five = scratch[:10]
+    rest = scratch[10:]
     per_level = len(rest) // 3
     gx, gy, gz = axes
     ix, iy, iz = (lax.axis_index(a) for a in ("gx", "gy", "gz"))
@@ -276,6 +278,7 @@
         chunks = [(0, half), (half, lp), (lp, lp + 1)] if index == 0 else [(0, lp + 1)]
         source = [raw.reshape(tiles + 1, nz * nx, LANES), approx_four, approx_five][index]
         levels.append(Level(index, lz, lx, lp, source, rest[index * per_level:(index + 1) * per_level],
+                            (one_ref, two_ref, three_ref)[index],
                             (send_sems, recv_sems), base, peers, chunks))
         base += 8 * len(chunks)
     first, second, third = levels
@@ -328,26 +331,14 @@
     second.prepare(0)
     second.send(0)
     first.all_lines([1, 2, 3])
-    store_one = pltpu.make_async_copy(first.staged, one_ref, out_sems.at[0])
-    store_one.start()
     second.receive(0)
     second.all_lines([0], approx_five)
 
     third.prepare(0)
     third.send(0)
     second.all_lines([1, 2, 3])
-    store_two = pltpu.make_async_copy(second.staged, two_ref, out_sems.at[1])
-    store_two.start()
     third.receive(0)
-    third.all_lines([0, 1, 2, 3], last)
-    store_three = pltpu.make_async_copy(third.staged, three_ref, out_sems.at[2])
-    store_three.start()
-    mz, mx = third.nz // 2, third.nx // 2
-    stores = [store_one, store_two, store_three]
-    for i in range(mz):
-        store = pltpu.make_async_copy(last.at[0, pl.ds(i * mx, mx)], approx_ref.at[i], out_sems.at[3 + i])
-        store.start()
-        stores.append(store)
+    third.all_lines([0, 1, 2, 3], approx_ref)
 
     for copy in y_copies:
         copy.wait_send()
@@ -355,8 +346,6 @@
         for copies in level.copies:
             for copy in copies:
                 copy.wait_send()
-    for store in stores:
-        store.wait()
 
 
 def solution(mesh):
@@ -374,32 +363,32 @@
             pltpu.SemaphoreType.DMA((n_sems,)),
             pltpu.SemaphoreType.DMA((n_sems,)),
             pltpu.SemaphoreType.DMA((tiles,)),
-            pltpu.SemaphoreType.DMA((3 + shapes[-1][0],)),
             pltpu.VMEM((tiles + 1, nz, nx, LANES), F32),
         ]
         scratch += [pltpu.VMEM(packed, F32)] * 4
-        for z, x, p in sizes:
+        for z, x, p in sizes[:2]:
             scratch.append(pltpu.VMEM((p + 1, z * x // 4, LANES), F32))
         for z, x, p in sizes:
             scratch += buffers(z, x, p)
         outs = [jax.ShapeDtypeStruct(shape, F32) for shape in shapes]
         results = pl.pallas_call(
             functools.partial(kernel, sizes, axes),
-            out_shape=outs,
+            out_shape=[pltpu.VMEM(shape, F32) for shape in shapes],
             in_specs=[pl.BlockSpec(memory_space=pltpu.HBM)],
-            out_specs=[pl.BlockSpec(memory_space=pl.ANY)] * 4,
+            out_specs=[pl.BlockSpec(memory_space=pltpu.VMEM)] * 4,
             scratch_shapes=scratch,
             compiler_params=pltpu.CompilerParams(
-                collective_id=0, has_side_effects=True, vmem_limit_bytes=40 << 20
+                collective_id=0, has_side_effects=True, vmem_limit_bytes=59 << 20
             ),
             cost_estimate=pl.CostEstimate(flops=20_000_000, bytes_accessed=2 << 20, transcendentals=0),
         )(density)
         return pl.pallas_call(
             hand_out,
             out_shape=outs,
-            in_specs=[pl.BlockSpec(memory_space=pl.ANY)] * 4,
+            in_specs=[pl.BlockSpec(memory_space=pltpu.VMEM)] * 4,
             out_specs=[pl.BlockSpec(memory_space=pltpu.HBM)] * 4,
             scratch_shapes=[pltpu.SemaphoreType.DMA((4,))],
+            compiler_params=pltpu.CompilerParams(vmem_limit_bytes=1 << 20),
             cost_estimate=pl.CostEstimate(flops=0, bytes_accessed=2 << 20, transcendentals=0),
         )(*results)
 

time: 65.6 us -> 29.6 us (0.45)
  Pallas kernels: 60.5 us -> 28.5 us
  local copies, waits for them, and re-layouts: 3.97 us -> 0 us
    pallas_call x1, Pallas kernels: 32.9 us -> 0.99 us  [on_device(): pl.pallas_call(hand_out, out_shape=outs, in_specs=[pl.BlockSpec(memory_sp...]
    unnamed x10 -> x0, local copies, waits for them, and re-layouts: 3.97 us -> none
where the time goes in v3:
time: 29.6 us; the launch traced here: 29.1 us
  Pallas kernels  28.5 us (96%)
  between operations  0.64 us (2%)
    pallas_call x1, Pallas kernels, on_device(): pl.pallas_call(functools.partial(kernel, sizes, axes), out_shape=[pltpu.V...  27.5 us
    pallas_call x1, Pallas kernels, on_device(): pl.pallas_call(hand_out, out_shape=outs, in_specs=[pl.BlockSpec(memory_sp...  0.99 us

profile of v3, /device:TPU:0, one launch (start us, length us, event | category | flops | bytes accessed | tf_op | source)
XLA Modules:
  0.0 29.1 jit_solution(9227061531664497136)
XLA Ops:
  0.6 27.5 %shard_map.46 = (f32[7,8,8,512]{3,2,1,0:T(8,128)S(1)}, f32[7,4,4,256]{3,2,1,0:T(4,128)S(1)}, f32[7,2,2,128]{3,2,1,0:T(2,128)S(1)}, f32[2,2,128]{2,1,0:T(2,128)S(1)}) custom-call(f32[16,16,1024]{2,1,0:T(8,128)} %u_ref.1), custom_call_target="tpu_custom_call" | custom-call | flops 20000000 | bytes 2097152 | tf_op jit(solution)/shard_map/pallas_call | solution.py:374
  28.1 1.0 %shard_map.47 = (f32[7,8,8,512]{3,2,1,0:T(8,128)}, f32[7,4,4,256]{3,2,1,0:T(4,128)}, f32[7,2,2,128]{3,2,1,0:T(2,128)}, f32[2,2,128]{2,1,0:T(2,128)}) custom-call(f32[7,8,8,512]{3,2,1,0:T(8,128)S(1)} %get-tuple-element.8.refs_0_, f32[7,4,4,256]{3,2,1,0:T(4,128)S(1)} %get-tuple-element.9.refs_1_, f32[7,2,2,128]{3,2,1,0:T(2,128)S(1)} %get-tuple-element.10.refs_2_, ...), custom_call_target="tpu_custom_call" | custom-call | bytes 2097152 | tf_op jit(solution)/shard_map/pallas_call | solution.py:385

commit v4 on v3

--- a/solution.py
+++ b/solution.py
@@ -54,6 +54,15 @@
     d = d + GAMMA * (s + after(s))
     s = s + DELTA * (before(d) + d)
     return s, d
+
+
+def circle(tiles):
+    ends = tiles[-1]
+    turned = pltpu.roll(ends, LANES // 2, 1)
+    near = lax.broadcasted_iota(jnp.int32, ends.shape, 1) < LANES // 2
+    even = jnp.concatenate(tiles[0:-1:2] + [jnp.where(near, ends, turned)], axis=1)
+    odd = jnp.concatenate(tiles[1:-1:2] + [jnp.where(near, turned, ends)], axis=1)
+    return even, odd
 
 
 def exact_select(x, choose):
@@ -188,13 +197,7 @@
         zb, xb = band // 2, band % 2
         mx = self.nx // 2
         rows = pl.ds(rows_from * mx, planes * mx)
-        ends = self.both[band, 2 * self.pairs, rows, :]
-        turned = pltpu.roll(ends, LANES // 2, 1)
-        near = lax.broadcasted_iota(jnp.int32, ends.shape, 1) < LANES // 2
-        evens = [self.both[band, 2 * j, rows, :] for j in range(self.pairs)]
-        odds = [self.both[band, 2 * j + 1, rows, :] for j in range(self.pairs)]
-        even = jnp.concatenate(evens + [jnp.where(near, ends, turned)], axis=1)
-        odd = jnp.concatenate(odds + [jnp.where(near, turned, ends)], axis=1)
+        even, odd = circle([self.both[band, t, rows, :] for t in range(2 * self.pairs + 1)])
         low, high = lift_lanes(even, odd)
         width = self.pairs * LANES
         low = low * ZETA ** (3 - 2 * (zb + xb))
@@ -219,6 +222,121 @@
                 self.lines(band, 0, step, approx)
 
 
+class FirstLevel:
+    def __init__(self, nz, nx, pairs, source, refs, details, sems, sem_base, peers, chunks):
+        self.nz, self.nx, self.pairs, self.source, self.details = nz, nx, pairs, source, details
+        self.split, self.xs, self.xr, self.own_x, self.flat, self.zs, self.zr = refs
+        self.chunks = chunks
+        send_sems, recv_sems = sems
+        moves = []
+        for c in range(len(chunks)):
+            start, stop = self.tile_range(c)
+            tiles = pl.ds(start, stop - start)
+            moves.append([(self.xs.at[s, tiles], self.xr.at[1 - s, tiles], peers["x"][s]) for s in (0, 1)])
+        for b in range(4):
+            tiles = pl.ds(0, self.band_tiles(b))
+            moves.append([
+                (self.zs.at[b, s, tiles], self.zr.at[b, 1 - s, tiles], peers["z"][s]) for s in (0, 1)
+            ])
+        self.copies = []
+        for k, pair in enumerate(moves):
+            self.copies.append([
+                pltpu.make_async_remote_copy(
+                    src_ref=src, dst_ref=dst,
+                    send_sem=send_sems.at[sem_base + 2 * k + i],
+                    recv_sem=recv_sems.at[sem_base + 2 * k + i],
+                    device_id=where, device_id_type=MESH,
+                )
+                for i, (src, dst, where) in enumerate(pair)
+            ])
+
+    tile_range = Level.tile_range
+    split_chunk = Level.split_chunk
+
+    def band_tiles(self, b):
+        return self.pairs + (1 if b == 0 else 0)
+
+    def tile_states(self, t):
+        states = boundary_states(lambda x: self.split[t, pl.ds(x, self.nz, stride=self.nx), :], self.nx)
+        for i, state in enumerate(states):
+            self.xs[i // 2, t, i % 2] = state
+
+    def prepare(self, c):
+        self.split_chunk(c)
+        pl.loop(*self.tile_range(c))(self.tile_states)
+
+    def start(self, k):
+        for copy in self.copies[k]:
+            copy.start()
+
+    def lift_x(self, t):
+        nz, nx = self.nz, self.nx
+        bands = lift(
+            lambda x: self.split[t, pl.ds(x, nz, stride=nx), :], nx,
+            (self.xr[0, t, 0], self.xr[0, t, 1]), (self.xr[1, t, 0], self.xr[1, t, 1]),
+        )
+        for band, lines in enumerate(bands):
+            for i, line in enumerate(lines):
+                self.own_x[band, t, pl.ds(i, nz, stride=nx // 2), :] = line
+
+    def receive_x(self, c):
+        for copy in self.copies[c]:
+            copy.wait_recv()
+        pl.loop(*self.tile_range(c))(self.lift_x)
+
+    def lift_y(self, xb):
+        count = self.nx
+
+        def some(k):
+            rows = pl.ds(pl.multiple_of(k * count, count), count)
+            even, odd = circle([self.own_x[xb, t, rows, :] for t in range(2 * self.pairs + 1)])
+            low, high = lift_lanes(even, odd)
+            for j in range(self.band_tiles(xb)):
+                self.flat[xb, j, rows, :] = low[:, j * LANES:(j + 1) * LANES]
+            for j in range(self.pairs):
+                self.flat[2 + xb, j, rows, :] = high[:, j * LANES:(j + 1) * LANES]
+
+        pl.loop(0, self.nz // 2)(some)
+
+    def send_z(self, b):
+        mx, n = self.nx // 2, self.band_tiles(b)
+        states = boundary_states(lambda z: self.flat[b, 0:n, z * mx:(z + 1) * mx, :], self.nz)
+        for i, state in enumerate(states):
+            self.zs[b, i // 2, 0:n, (i % 2) * mx:(i % 2 + 1) * mx, :] = state
+        self.start(len(self.chunks) + b)
+
+    def receive_z(self, b, approx=None):
+        mx = self.nx // 2
+        for copy in self.copies[len(self.chunks) + b]:
+            copy.wait_recv()
+
+        def tile(t, inside=True):
+            halo = [self.zr[b, s, t, i * mx:(i + 1) * mx, :] for s in (0, 1) for i in (0, 1)]
+            bands = lift(lambda z: self.flat[b, t, z * mx:(z + 1) * mx, :], self.nz, halo[:2], halo[2:])
+            for zb, lines in enumerate(bands):
+                scale = ZETA ** (3 - 2 * (zb + b // 2 + b % 2))
+                for i, line in enumerate(lines):
+                    if zb == 0 and b == 0:
+                        approx[t, i * mx:(i + 1) * mx, :] = line * scale
+                    elif inside:
+                        lanes = pl.ds(pl.multiple_of(t * LANES, LANES), LANES)
+                        self.details[4 * zb + b - 1, i, :, lanes] = line * scale
+
+        pl.loop(0, self.pairs)(tile)
+        if b == 0:
+            tile(self.pairs, inside=False)
+
+
+def first_buffers(nz, nx, pairs):
+    tiles = 2 * pairs + 1
+    shapes = [(tiles, nz * nx, LANES)]
+    shapes += [(2, tiles, 2, nz, LANES)] * 2
+    shapes += [(2, tiles, nz * nx // 2, LANES)]
+    shapes += [(4, pairs + 1, nz * nx // 2, LANES)]
+    shapes += [(4, 2, pairs + 1, nx, LANES)] * 2
+    return [pltpu.VMEM(shape, F32) for shape in shapes]
+
+
 def buffers(nz, nx, pairs):
     tiles = 2 * pairs + 1
     shapes = [(tiles, nz * nx, LANES)]
@@ -244,7 +362,8 @@
     scratch = list(scratch)
     send_sems, recv_sems, in_sems, raw, pack_l, pack_r, halo_l, halo_r, approx_four, approx_five = scratch[:10]
     rest = scratch[10:]
-    per_level = len(rest) // 3
+    first_refs, rest = rest[:7], rest[7:]
+    per_level = len(rest) // 2
     gx, gy, gz = axes
     ix, iy, iz = (lax.axis_index(a) for a in ("gx", "gy", "gz"))
     around = lambda i, n: (lax.rem(i + n - 1, n), lax.rem(i + 1, n))
@@ -272,16 +391,14 @@
         pl.semaphore_signal(barrier, inc=1, device_id=where, device_id_type=MESH)
 
     half = pairs // 2
-    levels = []
-    base = 2
-    for index, (lz, lx, lp) in enumerate(sizes):
-        chunks = [(0, half), (half, lp), (lp, lp + 1)] if index == 0 else [(0, lp + 1)]
-        source = [raw.reshape(tiles + 1, nz * nx, LANES), approx_four, approx_five][index]
-        levels.append(Level(index, lz, lx, lp, source, rest[index * per_level:(index + 1) * per_level],
-                            (one_ref, two_ref, three_ref)[index],
-                            (send_sems, recv_sems), base, peers, chunks))
-        base += 8 * len(chunks)
-    first, second, third = levels
+    sems = (send_sems, recv_sems)
+    chunks = [(0, half), (half, pairs), (pairs, pairs + 1)]
+    first = FirstLevel(nz, nx, pairs, raw.reshape(tiles + 1, nz * nx, LANES), first_refs, one_ref, sems, 2, peers, chunks)
+    second, third = (
+        Level(i, *sizes[i], source, rest[(i - 1) * per_level:i * per_level], details, sems, 8 + 8 * i, peers,
+              [(0, sizes[i][2] + 1)])
+        for i, source, details in ((1, approx_four, two_ref), (2, approx_five, three_ref))
+    )
 
     groups = LANES // HALO
     part = nz * nx // groups
@@ -311,9 +428,9 @@
     ]
     for copy in y_copies:
         copy.start()
-    first.send(0)
+    first.start(0)
     first.prepare(1)
-    first.send(1)
+    first.start(1)
     for copy in y_copies:
         copy.wait_recv()
     for g in range(groups):
@@ -323,26 +440,34 @@
             lane < HALO, after, jnp.where(lane >= LANES - HALO, before, 0.0)
         )
     first.prepare(2)
-    first.send(2)
+    first.start(2)
     for c in range(3):
-        first.receive(c)
-    first.all_lines([0], approx_four)
+        first.receive_x(c)
+    first.lift_y(0)
+    first.send_z(0)
+    first.send_z(2)
+    first.lift_y(1)
+    first.receive_z(0, approx_four)
 
     second.prepare(0)
     second.send(0)
-    first.all_lines([1, 2, 3])
+    first.send_z(1)
+    first.send_z(3)
+    first.receive_z(2)
     second.receive(0)
     second.all_lines([0], approx_five)
 
     third.prepare(0)
     third.send(0)
     second.all_lines([1, 2, 3])
+    first.receive_z(1)
+    first.receive_z(3)
     third.receive(0)
     third.all_lines([0, 1, 2, 3], approx_ref)
 
     for copy in y_copies:
         copy.wait_send()
-    for level in levels:
+    for level in (first, second, third):
         for copies in level.copies:
             for copy in copies:
                 copy.wait_send()
@@ -357,7 +482,7 @@
         tiles = ny // LANES
         shapes = [(7, z // 2, x // 2, p * LANES) for z, x, p in sizes]
         shapes.append(shapes[-1][1:])
-        n_sems = 2 + 8 * 5
+        n_sems = 32
         packed = (nz * nx * HALO // LANES, LANES)
         scratch = [
             pltpu.SemaphoreType.DMA((n_sems,)),
@@ -368,7 +493,8 @@
         scratch += [pltpu.VMEM(packed, F32)] * 4
         for z, x, p in sizes[:2]:
             scratch.append(pltpu.VMEM((p + 1, z * x // 4, LANES), F32))
-        for z, x, p in sizes:
+        scratch += first_buffers(*sizes[0])
+        for z, x, p in sizes[1:]:
             scratch += buffers(z, x, p)
         outs = [jax.ShapeDtypeStruct(shape, F32) for shape in shapes]
         results = pl.pallas_call(

time: 29.6 us -> 31.9 us (1.078)
  Pallas kernels: 28.5 us -> 30.9 us
    pallas_call x1, Pallas kernels: 27.5 us -> 29.9 us  [on_device(): pl.pallas_call(functools.partial(kernel, sizes, axes), out_shape=[pltpu.V...]
where the time goes in v4:
time: 31.9 us; the launch traced here: 31.5 us
  Pallas kernels  30.9 us (97%)
  between operations  0.64 us (2%)
    pallas_call x1, Pallas kernels, on_device(): pl.pallas_call(functools.partial(kernel, sizes, axes), out_shape=[pltpu.V...  29.9 us
    pallas_call x1, Pallas kernels, on_device(): pl.pallas_call(hand_out, out_shape=outs, in_specs=[pl.BlockSpec(memory_sp...  0.99 us

profile of v4, /device:TPU:0, one launch (start us, length us, event | category | flops | bytes accessed | tf_op | source)
XLA Modules:
  0.0 31.5 jit_solution(10005351784048081300)
XLA Ops:
  0.6 29.9 %shard_map.46 = (f32[7,8,8,512]{3,2,1,0:T(8,128)S(1)}, f32[7,4,4,256]{3,2,1,0:T(4,128)S(1)}, f32[7,2,2,128]{3,2,1,0:T(2,128)S(1)}, f32[2,2,128]{2,1,0:T(2,128)S(1)}) custom-call(f32[16,16,1024]{2,1,0:T(8,128)} %u_ref.1), custom_call_target="tpu_custom_call" | custom-call | flops 20000000 | bytes 2097152 | tf_op jit(solution)/shard_map/pallas_call | solution.py:500
  30.5 1.0 %shard_map.47 = (f32[7,8,8,512]{3,2,1,0:T(8,128)}, f32[7,4,4,256]{3,2,1,0:T(4,128)}, f32[7,2,2,128]{3,2,1,0:T(2,128)}, f32[2,2,128]{2,1,0:T(2,128)}) custom-call(f32[7,8,8,512]{3,2,1,0:T(8,128)S(1)} %get-tuple-element.8.refs_0_, f32[7,4,4,256]{3,2,1,0:T(4,128)S(1)} %get-tuple-element.9.refs_1_, f32[7,2,2,128]{3,2,1,0:T(2,128)S(1)} %get-tuple-element.10.refs_2_, ...), custom_call_target="tpu_custom_call" | custom-call | bytes 2097152 | tf_op jit(solution)/shard_map/pallas_call | solution.py:511

commit v5 on v4

--- a/solution.py
+++ b/solution.py
@@ -144,82 +144,67 @@
                 lane = lax.broadcasted_iota(jnp.int32, (rows, LANES), 1)
                 self.split[2 * j] = jnp.where(lane < LANES // 2, even, odd)
 
-    def tile_states(self, t):
-        nz, nx = self.nz, self.nx
-        states = boundary_states(lambda z: self.split[t, z * nx:(z + 1) * nx, :], nz)
-        for i, state in enumerate(states):
-            self.zs[t, i * nx:(i + 1) * nx, :] = state
-        states = boundary_states(lambda x: self.split[t, pl.ds(x, nz, stride=nx), :], nx)
-        for i, state in enumerate(states):
-            self.xs[i // 2, t, i % 2] = state
-        states = boundary_states(lambda x: self.zs[t, pl.ds(x, 4, stride=nx), :], nx)
-        for i, state in enumerate(states):
-            self.cs[i // 2, t, i % 2] = state
-
     def prepare(self, c):
         self.split_chunk(c)
-        pl.loop(*self.tile_range(c))(self.tile_states)
+        nz, nx = self.nz, self.nx
+        states = boundary_states(lambda z: self.split[:, z * nx:(z + 1) * nx, :], nz)
+        for i, state in enumerate(states):
+            self.zs[:, i * nx:(i + 1) * nx, :] = state
+        states = boundary_states(lambda x: self.split[:, pl.ds(x, nz, stride=nx), :], nx)
+        for i, state in enumerate(states):
+            self.xs[i // 2, :, i % 2] = state
+        states = boundary_states(lambda x: self.zs[:, pl.ds(x, 4, stride=nx), :], nx)
+        for i, state in enumerate(states):
+            self.cs[i // 2, :, i % 2] = state
 
     def send(self, c):
         for copy in self.copies[c]:
             copy.start()
 
-    def tile_planes(self, t):
-        nz, nx = self.nz, self.nx
-        mx = nx // 2
-        bands = lift(
-            lambda x: self.split[t, pl.ds(x, nz, stride=nx), :], nx,
-            (self.xr[0, t, 0], self.xr[0, t, 1]), (self.xr[1, t, 0], self.xr[1, t, 1]),
-        )
-        for band, lines in enumerate(bands):
-            for i, line in enumerate(lines):
-                self.own_x[band, t, pl.ds(i, nz, stride=mx), :] = line
-        bands = lift(
-            lambda x: self.zr[t, pl.ds(x, 4, stride=nx), :], nx,
-            (self.cr[0, t, 0], self.cr[0, t, 1]), (self.cr[1, t, 0], self.cr[1, t, 1]),
-        )
-        for band, lines in enumerate(bands):
-            for i, line in enumerate(lines):
-                self.halo_x[band, t, pl.ds(i, 4, stride=mx), :] = line
-        for xb in (0, 1):
-            halo = [self.halo_x[xb, t, i * mx:(i + 1) * mx, :] for i in range(4)]
-            bands = lift(lambda z: self.own_x[xb, t, z * mx:(z + 1) * mx, :], nz, halo[:2], halo[2:])
-            for zb, lines in enumerate(bands):
-                for i, line in enumerate(lines):
-                    self.both[2 * zb + xb, t, i * mx:(i + 1) * mx, :] = line
-
     def receive(self, c):
         for copy in self.copies[c]:
             copy.wait_recv()
-        pl.loop(*self.tile_range(c))(self.tile_planes)
-
-    def lines(self, band, rows_from, planes, approx):
-        zb, xb = band // 2, band % 2
-        mx = self.nx // 2
-        rows = pl.ds(rows_from * mx, planes * mx)
-        even, odd = circle([self.both[band, t, rows, :] for t in range(2 * self.pairs + 1)])
-        low, high = lift_lanes(even, odd)
+        nz, nx = self.nz, self.nx
+        mx = nx // 2
+        band_rows = nz * nx // 4
+        for ref, n, source, ends in ((self.own_x, nz, self.split, self.xr), (self.halo_x, 4, self.zr, self.cr)):
+            bands = lift(
+                lambda x: source[:, pl.ds(x, n, stride=nx), :], nx,
+                (ends[0, :, 0], ends[0, :, 1]), (ends[1, :, 0], ends[1, :, 1]),
+            )
+            for band, lines in enumerate(bands):
+                for i, line in enumerate(lines):
+                    ref[band, :, pl.ds(i, n, stride=mx), :] = line
+        for xb in (0, 1):
+            halo = [self.halo_x[xb, :, i * mx:(i + 1) * mx, :] for i in range(4)]
+            bands = lift(lambda z: self.own_x[xb, :, z * mx:(z + 1) * mx, :], nz, halo[:2], halo[2:])
+            for zb, lines in enumerate(bands):
+                for i, line in enumerate(lines):
+                    row = (2 * zb + xb) * band_rows + i * mx
+                    self.both[:, row:row + mx, :] = line
+
+    def lines(self, bands, approx=None):
+        mx, mz = self.nx // 2, self.nz // 2
+        band_rows = mx * mz
+        first, last = bands[0], bands[-1] + 1
+        even, odd = circle([self.both[t, first * band_rows:last * band_rows, :] for t in range(2 * self.pairs + 1)])
+        lows, highs = lift_lanes(even, odd)
         width = self.pairs * LANES
-        low = low * ZETA ** (3 - 2 * (zb + xb))
-        high = high[:, :width] * ZETA ** (1 - 2 * (zb + xb))
-        if band == 0 and self.index < 2:
-            for j in range(self.pairs + 1):
-                approx[j, rows, :] = low[:, j * LANES:(j + 1) * LANES]
-        for i in range(planes):
-            if band == 0 and self.index == 2:
-                approx[rows_from + i] = low[i * mx:(i + 1) * mx, :width]
-            if band > 0:
-                self.details[4 * zb + xb - 1, rows_from + i] = low[i * mx:(i + 1) * mx, :width]
-            self.details[4 * zb + 2 + xb - 1, rows_from + i] = high[i * mx:(i + 1) * mx]
-
-    def all_lines(self, bands, approx=None):
-        planes = self.nz // 2
-        step = min(planes, 2)
-        for band in bands:
-            if planes // step > 1:
-                pl.loop(0, planes // step)(lambda k, band=band: self.lines(band, k * step, step, approx))
-            else:
-                self.lines(band, 0, step, approx)
+        for k, band in enumerate(bands):
+            zb, xb = band // 2, band % 2
+            rows = slice(k * band_rows, (k + 1) * band_rows)
+            low = lows[rows] * ZETA ** (3 - 2 * (zb + xb))
+            high = highs[rows, :width] * ZETA ** (1 - 2 * (zb + xb))
+            if band == 0 and self.index < 2:
+                for j in range(self.pairs + 1):
+                    approx[j] = low[:, j * LANES:(j + 1) * LANES]
+            for i in range(mz):
+                row = low[i * mx:(i + 1) * mx, :width]
+                if band > 0:
+                    self.details[4 * zb + xb - 1, i] = row
+                elif self.index == 2:
+                    approx[i] = row
+                self.details[4 * zb + 2 + xb - 1, i] = high[i * mx:(i + 1) * mx]
 
 
 class FirstLevel:
@@ -256,14 +241,12 @@
     def band_tiles(self, b):
         return self.pairs + (1 if b == 0 else 0)
 
-    def tile_states(self, t):
-        states = boundary_states(lambda x: self.split[t, pl.ds(x, self.nz, stride=self.nx), :], self.nx)
-        for i, state in enumerate(states):
-            self.xs[i // 2, t, i % 2] = state
-
     def prepare(self, c):
         self.split_chunk(c)
-        pl.loop(*self.tile_range(c))(self.tile_states)
+        start, stop = self.tile_range(c)
+        states = boundary_states(lambda x: self.split[start:stop, pl.ds(x, self.nz, stride=self.nx), :], self.nx)
+        for i, state in enumerate(states):
+            self.xs[i // 2, start:stop, i % 2] = state
 
     def start(self, k):
         for copy in self.copies[k]:
@@ -282,10 +265,11 @@
     def receive_x(self, c):
         for copy in self.copies[c]:
             copy.wait_recv()
-        pl.loop(*self.tile_range(c))(self.lift_x)
+        start, stop = self.tile_range(c)
+        pl.loop(start, stop, unroll=min(2, stop - start))(self.lift_x)
 
     def lift_y(self, xb):
-        count = self.nx
+        count = self.nx * self.nz // 4
 
         def some(k):
             rows = pl.ds(pl.multiple_of(k * count, count), count)
@@ -296,7 +280,7 @@
             for j in range(self.pairs):
                 self.flat[2 + xb, j, rows, :] = high[:, j * LANES:(j + 1) * LANES]
 
-        pl.loop(0, self.nz // 2)(some)
+        pl.loop(0, 2)(some)
 
     def send_z(self, b):
         mx, n = self.nx // 2, self.band_tiles(b)
@@ -310,21 +294,17 @@
         for copy in self.copies[len(self.chunks) + b]:
             copy.wait_recv()
 
-        def tile(t, inside=True):
-            halo = [self.zr[b, s, t, i * mx:(i + 1) * mx, :] for s in (0, 1) for i in (0, 1)]
-            bands = lift(lambda z: self.flat[b, t, z * mx:(z + 1) * mx, :], self.nz, halo[:2], halo[2:])
-            for zb, lines in enumerate(bands):
-                scale = ZETA ** (3 - 2 * (zb + b // 2 + b % 2))
-                for i, line in enumerate(lines):
-                    if zb == 0 and b == 0:
-                        approx[t, i * mx:(i + 1) * mx, :] = line * scale
-                    elif inside:
-                        lanes = pl.ds(pl.multiple_of(t * LANES, LANES), LANES)
-                        self.details[4 * zb + b - 1, i, :, lanes] = line * scale
-
-        pl.loop(0, self.pairs)(tile)
-        if b == 0:
-            tile(self.pairs, inside=False)
+        n = self.band_tiles(b)
+        halo = [self.zr[b, s, 0:n, i * mx:(i + 1) * mx, :] for s in (0, 1) for i in (0, 1)]
+        bands = lift(lambda z: self.flat[b, 0:n, z * mx:(z + 1) * mx, :], self.nz, halo[:2], halo[2:])
+        for zb, lines in enumerate(bands):
+            scale = ZETA ** (3 - 2 * (zb + b // 2 + b % 2))
+            for i, line in enumerate(lines):
+                line = line * scale
+                if zb == 0 and b == 0:
+                    approx[:, i * mx:(i + 1) * mx, :] = line
+                else:
+                    self.details[4 * zb + b - 1, i] = jnp.concatenate([line[t] for t in range(self.pairs)], axis=1)
 
 
 def first_buffers(nz, nx, pairs):
@@ -344,7 +324,7 @@
     shapes += [(2, tiles, 2, nz, LANES)] * 2
     shapes += [(2, tiles, 2, 4, LANES)] * 2
     shapes += [(2, tiles, nz * nx // 2, LANES), (2, tiles, 2 * nx, LANES)]
-    shapes += [(4, tiles, nz * nx // 4, LANES)]
+    shapes += [(tiles, nz * nx, LANES)]
     return [pltpu.VMEM(shape, F32) for shape in shapes]
 
 
@@ -455,15 +435,15 @@
     first.send_z(3)
     first.receive_z(2)
     second.receive(0)
-    second.all_lines([0], approx_five)
+    second.lines([0], approx_five)
 
     third.prepare(0)
     third.send(0)
-    second.all_lines([1, 2, 3])
+    second.lines([1, 2, 3])
     first.receive_z(1)
     first.receive_z(3)
     third.receive(0)
-    third.all_lines([0, 1, 2, 3], approx_ref)
+    third.lines([0, 1, 2, 3], approx_ref)
 
     for copy in y_copies:
         copy.wait_send()

time: 31.9 us -> 28.9 us (0.906)
  Pallas kernels: 30.9 us -> 27.9 us
    pallas_call x1, Pallas kernels: 29.9 us -> 26.9 us  [on_device(): pl.pallas_call(functools.partial(kernel, sizes, axes), out_shape=[pltpu.V...]
where the time goes in v5:
time: 28.9 us; the launch traced here: 28.6 us
  Pallas kernels  27.9 us (97%)
  between operations  0.64 us (2%)
    pallas_call x1, Pallas kernels, on_device(): pl.pallas_call(functools.partial(kernel, sizes, axes), out_shape=[pltpu.V...  26.9 us
    pallas_call x1, Pallas kernels, on_device(): pl.pallas_call(hand_out, out_shape=outs, in_specs=[pl.BlockSpec(memory_sp...  0.99 us

profile of v5, /device:TPU:0, one launch (start us, length us, event | category | flops | bytes accessed | tf_op | source)
XLA Modules:
  0.0 28.6 jit_solution(1155539197978840003)
XLA Ops:
  0.6 26.9 %shard_map.46 = (f32[7,8,8,512]{3,2,1,0:T(8,128)S(1)}, f32[7,4,4,256]{3,2,1,0:T(4,128)S(1)}, f32[7,2,2,128]{3,2,1,0:T(2,128)S(1)}, f32[2,2,128]{2,1,0:T(2,128)S(1)}) custom-call(f32[16,16,1024]{2,1,0:T(8,128)} %u_ref.1), custom_call_target="tpu_custom_call" | custom-call | flops 20000000 | bytes 2097152 | tf_op jit(solution)/shard_map/pallas_call | solution.py:480
  27.6 1.0 %shard_map.47 = (f32[7,8,8,512]{3,2,1,0:T(8,128)}, f32[7,4,4,256]{3,2,1,0:T(4,128)}, f32[7,2,2,128]{3,2,1,0:T(2,128)}, f32[2,2,128]{2,1,0:T(2,128)}) custom-call(f32[7,8,8,512]{3,2,1,0:T(8,128)S(1)} %get-tuple-element.8.refs_0_, f32[7,4,4,256]{3,2,1,0:T(4,128)S(1)} %get-tuple-element.9.refs_1_, f32[7,2,2,128]{3,2,1,0:T(2,128)S(1)} %get-tuple-element.10.refs_2_, ...), custom_call_target="tpu_custom_call" | custom-call | bytes 2097152 | tf_op jit(solution)/shard_map/pallas_call | solution.py:491

commit v6 on v5

--- a/solution.py
+++ b/solution.py
@@ -210,7 +210,7 @@
 class FirstLevel:
     def __init__(self, nz, nx, pairs, source, refs, details, sems, sem_base, peers, chunks):
         self.nz, self.nx, self.pairs, self.source, self.details = nz, nx, pairs, source, details
-        self.split, self.xs, self.xr, self.own_x, self.flat, self.zs, self.zr = refs
+        self.split, self.xs, self.xr, self.xe, self.own_x, self.flat, self.zs, self.zr = refs
         self.chunks = chunks
         send_sems, recv_sems = sems
         moves = []
@@ -241,12 +241,30 @@
     def band_tiles(self, b):
         return self.pairs + (1 if b == 0 else 0)
 
-    def prepare(self, c):
-        self.split_chunk(c)
-        start, stop = self.tile_range(c)
-        states = boundary_states(lambda x: self.split[start:stop, pl.ds(x, self.nz, stride=self.nx), :], self.nx)
+    def states(self, start, stop):
+        states = boundary_states(lambda x: self.source[start:stop, pl.ds(x, self.nz, stride=self.nx), :], self.nx)
         for i, state in enumerate(states):
             self.xs[i // 2, start:stop, i % 2] = state
+
+    def split_states(self, c):
+        start, stop = self.chunks[c]
+        rows = 2 * self.nz
+        take = lambda side, t: self.xr[side, t].reshape(rows, LANES)
+        if start == self.pairs:
+            x = jnp.concatenate([take(side, 2 * start) for side in (0, 1)], axis=0)
+            both = exact_select(x, split_matrix(LANES))
+            for side in (0, 1):
+                self.xe[side, 2 * start] = both[side * rows:(side + 1) * rows].reshape(2, self.nz, LANES)
+            return
+        order = [(side, j) for j in range(start, stop) for side in (0, 1)]
+        x = jnp.concatenate([
+            jnp.concatenate([take(side, 2 * j + odd) for side, j in order], axis=0) for odd in (0, 1)
+        ], axis=1)
+        both = exact_select(x, split_matrix(2 * LANES))
+        for i, (side, j) in enumerate(order):
+            for odd in (0, 1):
+                part = both[i * rows:(i + 1) * rows, odd * LANES:(odd + 1) * LANES]
+                self.xe[side, 2 * j + odd] = part.reshape(2, self.nz, LANES)
 
     def start(self, k):
         for copy in self.copies[k]:
@@ -256,7 +274,7 @@
         nz, nx = self.nz, self.nx
         bands = lift(
             lambda x: self.split[t, pl.ds(x, nz, stride=nx), :], nx,
-            (self.xr[0, t, 0], self.xr[0, t, 1]), (self.xr[1, t, 0], self.xr[1, t, 1]),
+            (self.xe[0, t, 0], self.xe[0, t, 1]), (self.xe[1, t, 0], self.xe[1, t, 1]),
         )
         for band, lines in enumerate(bands):
             for i, line in enumerate(lines):
@@ -265,6 +283,7 @@
     def receive_x(self, c):
         for copy in self.copies[c]:
             copy.wait_recv()
+        self.split_states(c)
         start, stop = self.tile_range(c)
         pl.loop(start, stop, unroll=min(2, stop - start))(self.lift_x)
 
@@ -310,7 +329,7 @@
 def first_buffers(nz, nx, pairs):
     tiles = 2 * pairs + 1
     shapes = [(tiles, nz * nx, LANES)]
-    shapes += [(2, tiles, 2, nz, LANES)] * 2
+    shapes += [(2, tiles, 2, nz, LANES)] * 3
     shapes += [(2, tiles, nz * nx // 2, LANES)]
     shapes += [(4, pairs + 1, nz * nx // 2, LANES)]
     shapes += [(4, 2, pairs + 1, nx, LANES)] * 2
@@ -342,7 +361,7 @@
     scratch = list(scratch)
     send_sems, recv_sems, in_sems, raw, pack_l, pack_r, halo_l, halo_r, approx_four, approx_five = scratch[:10]
     rest = scratch[10:]
-    first_refs, rest = rest[:7], rest[7:]
+    first_refs, rest = rest[:8], rest[8:]
     per_level = len(rest) // 2
     gx, gy, gz = axes
     ix, iy, iz = (lax.axis_index(a) for a in ("gx", "gy", "gz"))
@@ -396,10 +415,6 @@
 
     pack_l[...] = gather(0, 0)
     pack_r[...] = gather(tiles - 1, LANES - HALO)
-    for t in range(1, tiles - 1):
-        loads[t].wait()
-    first.prepare(0)
-
     pl.semaphore_wait(barrier, len(greeted))
     y_copies = [
         pltpu.make_async_remote_copy(src_ref=src, dst_ref=dst, send_sem=send_sems.at[i], recv_sem=recv_sems.at[i],
@@ -408,9 +423,13 @@
     ]
     for copy in y_copies:
         copy.start()
+    for t in range(1, tiles - 1):
+        loads[t].wait()
+    first.states(0, 2 * half)
     first.start(0)
-    first.prepare(1)
+    first.states(2 * half, tiles)
     first.start(1)
+    first.split_chunk(0)
     for copy in y_copies:
         copy.wait_recv()
     for g in range(groups):
@@ -419,8 +438,10 @@
         flat[tiles, g * part:(g + 1) * part, :] = jnp.where(
             lane < HALO, after, jnp.where(lane >= LANES - HALO, before, 0.0)
         )
-    first.prepare(2)
+    first.states(tiles, tiles + 1)
     first.start(2)
+    first.split_chunk(1)
+    first.split_chunk(2)
     for c in range(3):
         first.receive_x(c)
     first.lift_y(0)

time: 28.9 us -> 29.1 us (level)
  Pallas kernels: 27.9 us -> 28.3 us
    pallas_call x1, Pallas kernels: 26.9 us -> 27.3 us  [on_device(): pl.pallas_call(functools.partial(kernel, sizes, axes), out_shape=[pltpu.V...]
where the time goes in v6:
time: 29.1 us; the launch traced here: 28.9 us
  Pallas kernels  28.3 us (97%)
  between operations  0.64 us (2%)
    pallas_call x1, Pallas kernels, on_device(): pl.pallas_call(functools.partial(kernel, sizes, axes), out_shape=[pltpu.V...  27.3 us
    pallas_call x1, Pallas kernels, on_device(): pl.pallas_call(hand_out, out_shape=outs, in_specs=[pl.BlockSpec(memory_sp...  0.99 us

profile of v6, /device:TPU:0, one launch (start us, length us, event | category | flops | bytes accessed | tf_op | source)
XLA Modules:
  0.0 28.9 jit_solution(11605083169396517615)
XLA Ops:
  0.6 27.3 %shard_map.46 = (f32[7,8,8,512]{3,2,1,0:T(8,128)S(1)}, f32[7,4,4,256]{3,2,1,0:T(4,128)S(1)}, f32[7,2,2,128]{3,2,1,0:T(2,128)S(1)}, f32[2,2,128]{2,1,0:T(2,128)S(1)}) custom-call(f32[16,16,1024]{2,1,0:T(8,128)} %u_ref.1), custom_call_target="tpu_custom_call" | custom-call | flops 20000000 | bytes 2097152 | tf_op jit(solution)/shard_map/pallas_call | solution.py:501
  28.0 1.0 %shard_map.47 = (f32[7,8,8,512]{3,2,1,0:T(8,128)}, f32[7,4,4,256]{3,2,1,0:T(4,128)}, f32[7,2,2,128]{3,2,1,0:T(2,128)}, f32[2,2,128]{2,1,0:T(2,128)}) custom-call(f32[7,8,8,512]{3,2,1,0:T(8,128)S(1)} %get-tuple-element.8.refs_0_, f32[7,4,4,256]{3,2,1,0:T(4,128)S(1)} %get-tuple-element.9.refs_1_, f32[7,2,2,128]{3,2,1,0:T(2,128)S(1)} %get-tuple-element.10.refs_2_, ...), custom_call_target="tpu_custom_call" | custom-call | bytes 2097152 | tf_op jit(solution)/shard_map/pallas_call | solution.py:512

commit v7 on v6

--- a/solution.py
+++ b/solution.py
@@ -301,11 +301,13 @@
 
         pl.loop(0, 2)(some)
 
-    def send_z(self, b):
+    def states_z(self, b):
         mx, n = self.nx // 2, self.band_tiles(b)
         states = boundary_states(lambda z: self.flat[b, 0:n, z * mx:(z + 1) * mx, :], self.nz)
         for i, state in enumerate(states):
             self.zs[b, i // 2, 0:n, (i % 2) * mx:(i % 2 + 1) * mx, :] = state
+
+    def send_z(self, b):
         self.start(len(self.chunks) + b)
 
     def receive_z(self, b, approx=None):
@@ -445,17 +447,21 @@
     for c in range(3):
         first.receive_x(c)
     first.lift_y(0)
+    first.states_z(0)
     first.send_z(0)
+    first.lift_y(1)
+    first.states_z(2)
     first.send_z(2)
-    first.lift_y(1)
     first.receive_z(0, approx_four)
 
     second.prepare(0)
     second.send(0)
+    first.states_z(1)
+    first.states_z(3)
+    first.receive_z(2)
     first.send_z(1)
+    second.receive(0)
     first.send_z(3)
-    first.receive_z(2)
-    second.receive(0)
     second.lines([0], approx_five)
 
     third.prepare(0)

time: 29.1 us -> 29.5 us (1.014)
  Pallas kernels: 28.3 us -> 28.7 us
    pallas_call x1, Pallas kernels: 27.3 us -> 27.7 us  [on_device(): pl.pallas_call(functools.partial(kernel, sizes, axes), out_shape=[pltpu.V...]
where the time goes in v7:
time: 29.5 us; the launch traced here: 29.4 us
  Pallas kernels  28.7 us (97%)
  between operations  0.64 us (2%)
    pallas_call x1, Pallas kernels, on_device(): pl.pallas_call(functools.partial(kernel, sizes, axes), out_shape=[pltpu.V...  27.7 us
    pallas_call x1, Pallas kernels, on_device(): pl.pallas_call(hand_out, out_shape=outs, in_specs=[pl.BlockSpec(memory_sp...  0.99 us

profile of v7, /device:TPU:0, one launch (start us, length us, event | category | flops | bytes accessed | tf_op | source)
XLA Modules:
  0.0 29.4 jit_solution(15858535637415359984)
XLA Ops:
  0.6 27.7 %shard_map.46 = (f32[7,8,8,512]{3,2,1,0:T(8,128)S(1)}, f32[7,4,4,256]{3,2,1,0:T(4,128)S(1)}, f32[7,2,2,128]{3,2,1,0:T(2,128)S(1)}, f32[2,2,128]{2,1,0:T(2,128)S(1)}) custom-call(f32[16,16,1024]{2,1,0:T(8,128)} %u_ref.1), custom_call_target="tpu_custom_call" | custom-call | flops 20000000 | bytes 2097152 | tf_op jit(solution)/shard_map/pallas_call | solution.py:507
  28.4 1.0 %shard_map.47 = (f32[7,8,8,512]{3,2,1,0:T(8,128)}, f32[7,4,4,256]{3,2,1,0:T(4,128)}, f32[7,2,2,128]{3,2,1,0:T(2,128)}, f32[2,2,128]{2,1,0:T(2,128)}) custom-call(f32[7,8,8,512]{3,2,1,0:T(8,128)S(1)} %get-tuple-element.8.refs_0_, f32[7,4,4,256]{3,2,1,0:T(4,128)S(1)} %get-tuple-element.9.refs_1_, f32[7,2,2,128]{3,2,1,0:T(2,128)S(1)} %get-tuple-element.10.refs_2_, ...), custom_call_target="tpu_custom_call" | custom-call | bytes 2097152 | tf_op jit(solution)/shard_map/pallas_call | solution.py:518

commit v8 on v3

--- a/solution.py
+++ b/solution.py
@@ -54,6 +54,15 @@
     d = d + GAMMA * (s + after(s))
     s = s + DELTA * (before(d) + d)
     return s, d
+
+
+def circle(tiles):
+    ends = tiles[-1]
+    turned = pltpu.roll(ends, LANES // 2, 1)
+    near = lax.broadcasted_iota(jnp.int32, ends.shape, 1) < LANES // 2
+    even = jnp.concatenate(tiles[0:-1:2] + [jnp.where(near, ends, turned)], axis=1)
+    odd = jnp.concatenate(tiles[1:-1:2] + [jnp.where(near, turned, ends)], axis=1)
+    return even, odd
 
 
 def exact_select(x, choose):
@@ -135,6 +144,70 @@
                 lane = lax.broadcasted_iota(jnp.int32, (rows, LANES), 1)
                 self.split[2 * j] = jnp.where(lane < LANES // 2, even, odd)
 
+    def prepare(self, c):
+        self.split_chunk(c)
+        nz, nx = self.nz, self.nx
+        states = boundary_states(lambda z: self.split[:, z * nx:(z + 1) * nx, :], nz)
+        for i, state in enumerate(states):
+            self.zs[:, i * nx:(i + 1) * nx, :] = state
+        states = boundary_states(lambda x: self.split[:, pl.ds(x, nz, stride=nx), :], nx)
+        for i, state in enumerate(states):
+            self.xs[i // 2, :, i % 2] = state
+        states = boundary_states(lambda x: self.zs[:, pl.ds(x, 4, stride=nx), :], nx)
+        for i, state in enumerate(states):
+            self.cs[i // 2, :, i % 2] = state
+
+    def send(self, c):
+        for copy in self.copies[c]:
+            copy.start()
+
+    def receive(self, c):
+        for copy in self.copies[c]:
+            copy.wait_recv()
+        nz, nx = self.nz, self.nx
+        mx = nx // 2
+        band_rows = nz * nx // 4
+        for ref, n, source, ends in ((self.own_x, nz, self.split, self.xr), (self.halo_x, 4, self.zr, self.cr)):
+            bands = lift(
+                lambda x: source[:, pl.ds(x, n, stride=nx), :], nx,
+                (ends[0, :, 0], ends[0, :, 1]), (ends[1, :, 0], ends[1, :, 1]),
+            )
+            for band, lines in enumerate(bands):
+                for i, line in enumerate(lines):
+                    ref[band, :, pl.ds(i, n, stride=mx), :] = line
+        for xb in (0, 1):
+            halo = [self.halo_x[xb, :, i * mx:(i + 1) * mx, :] for i in range(4)]
+            bands = lift(lambda z: self.own_x[xb, :, z * mx:(z + 1) * mx, :], nz, halo[:2], halo[2:])
+            for zb, lines in enumerate(bands):
+                for i, line in enumerate(lines):
+                    row = (2 * zb + xb) * band_rows + i * mx
+                    self.both[:, row:row + mx, :] = line
+
+    def lines(self, bands, approx=None):
+        mx, mz = self.nx // 2, self.nz // 2
+        band_rows = mx * mz
+        first, last = bands[0], bands[-1] + 1
+        even, odd = circle([self.both[t, first * band_rows:last * band_rows, :] for t in range(2 * self.pairs + 1)])
+        lows, highs = lift_lanes(even, odd)
+        width = self.pairs * LANES
+        for k, band in enumerate(bands):
+            zb, xb = band // 2, band % 2
+            rows = slice(k * band_rows, (k + 1) * band_rows)
+            low = lows[rows] * ZETA ** (3 - 2 * (zb + xb))
+            high = highs[rows, :width] * ZETA ** (1 - 2 * (zb + xb))
+            if band == 0 and self.index < 2:
+                for j in range(self.pairs + 1):
+                    approx[j] = low[:, j * LANES:(j + 1) * LANES]
+            for i in range(mz):
+                row = low[i * mx:(i + 1) * mx, :width]
+                if band > 0:
+                    self.details[4 * zb + xb - 1, i] = row
+                elif self.index == 2:
+                    approx[i] = row
+                self.details[4 * zb + 2 + xb - 1, i] = high[i * mx:(i + 1) * mx]
+
+
+class FirstLevel(Level):
     def tile_states(self, t):
         nz, nx = self.nz, self.nx
         states = boundary_states(lambda z: self.split[t, z * nx:(z + 1) * nx, :], nz)
@@ -149,11 +222,8 @@
 
     def prepare(self, c):
         self.split_chunk(c)
-        pl.loop(*self.tile_range(c))(self.tile_states)
-
-    def send(self, c):
-        for copy in self.copies[c]:
-            copy.start()
+        start, stop = self.tile_range(c)
+        pl.loop(start, stop, unroll=min(2, stop - start))(self.tile_states)
 
     def tile_planes(self, t):
         nz, nx = self.nz, self.nx
@@ -177,46 +247,14 @@
             bands = lift(lambda z: self.own_x[xb, t, z * mx:(z + 1) * mx, :], nz, halo[:2], halo[2:])
             for zb, lines in enumerate(bands):
                 for i, line in enumerate(lines):
-                    self.both[2 * zb + xb, t, i * mx:(i + 1) * mx, :] = line
+                    row = (2 * zb + xb) * (nz * nx // 4) + i * mx
+                    self.both[t, row:row + mx, :] = line
 
     def receive(self, c):
         for copy in self.copies[c]:
             copy.wait_recv()
-        pl.loop(*self.tile_range(c))(self.tile_planes)
-
-    def lines(self, band, rows_from, planes, approx):
-        zb, xb = band // 2, band % 2
-        mx = self.nx // 2
-        rows = pl.ds(rows_from * mx, planes * mx)
-        ends = self.both[band, 2 * self.pairs, rows, :]
-        turned = pltpu.roll(ends, LANES // 2, 1)
-        near = lax.broadcasted_iota(jnp.int32, ends.shape, 1) < LANES // 2
-        evens = [self.both[band, 2 * j, rows, :] for j in range(self.pairs)]
-        odds = [self.both[band, 2 * j + 1, rows, :] for j in range(self.pairs)]
-        even = jnp.concatenate(evens + [jnp.where(near, ends, turned)], axis=1)
-        odd = jnp.concatenate(odds + [jnp.where(near, turned, ends)], axis=1)
-        low, high = lift_lanes(even, odd)
-        width = self.pairs * LANES
-        low = low * ZETA ** (3 - 2 * (zb + xb))
-        high = high[:, :width] * ZETA ** (1 - 2 * (zb + xb))
-        if band == 0 and self.index < 2:
-            for j in range(self.pairs + 1):
-                approx[j, rows, :] = low[:, j * LANES:(j + 1) * LANES]
-        for i in range(planes):
-            if band == 0 and self.index == 2:
-                approx[rows_from + i] = low[i * mx:(i + 1) * mx, :width]
-            if band > 0:
-                self.details[4 * zb + xb - 1, rows_from + i] = low[i * mx:(i + 1) * mx, :width]
-            self.details[4 * zb + 2 + xb - 1, rows_from + i] = high[i * mx:(i + 1) * mx]
-
-    def all_lines(self, bands, approx=None):
-        planes = self.nz // 2
-        step = min(planes, 2)
-        for band in bands:
-            if planes // step > 1:
-                pl.loop(0, planes // step)(lambda k, band=band: self.lines(band, k * step, step, approx))
-            else:
-                self.lines(band, 0, step, approx)
+        start, stop = self.tile_range(c)
+        pl.loop(start, stop, unroll=min(2, stop - start))(self.tile_planes)
 
 
 def buffers(nz, nx, pairs):
@@ -226,7 +264,7 @@
     shapes += [(2, tiles, 2, nz, LANES)] * 2
     shapes += [(2, tiles, 2, 4, LANES)] * 2
     shapes += [(2, tiles, nz * nx // 2, LANES), (2, tiles, 2 * nx, LANES)]
-    shapes += [(4, tiles, nz * nx // 4, LANES)]
+    shapes += [(tiles, nz * nx, LANES)]
     return [pltpu.VMEM(shape, F32) for shape in shapes]
 
 
@@ -272,16 +310,15 @@
         pl.semaphore_signal(barrier, inc=1, device_id=where, device_id_type=MESH)
 
     half = pairs // 2
-    levels = []
-    base = 2
-    for index, (lz, lx, lp) in enumerate(sizes):
-        chunks = [(0, half), (half, lp), (lp, lp + 1)] if index == 0 else [(0, lp + 1)]
-        source = [raw.reshape(tiles + 1, nz * nx, LANES), approx_four, approx_five][index]
-        levels.append(Level(index, lz, lx, lp, source, rest[index * per_level:(index + 1) * per_level],
-                            (one_ref, two_ref, three_ref)[index],
-                            (send_sems, recv_sems), base, peers, chunks))
-        base += 8 * len(chunks)
-    first, second, third = levels
+    sems = (send_sems, recv_sems)
+    chunks = [(0, half), (half, pairs), (pairs, pairs + 1)]
+    source = raw.reshape(tiles + 1, nz * nx, LANES)
+    first = FirstLevel(0, nz, nx, pairs, source, rest[:per_level], one_ref, sems, 2, peers, chunks)
+    second, third = (
+        Level(i, *sizes[i], source, rest[i * per_level:(i + 1) * per_level], details, sems, 18 + 8 * i, peers,
+              [(0, sizes[i][2] + 1)])
+        for i, source, details in ((1, approx_four, two_ref), (2, approx_five, three_ref))
+    )
 
     groups = LANES // HALO
     part = nz * nx // groups
@@ -299,10 +336,6 @@
 
     pack_l[...] = gather(0, 0)
     pack_r[...] = gather(tiles - 1, LANES - HALO)
-    for t in range(1, tiles - 1):
-        loads[t].wait()
-    first.prepare(0)
-
     pl.semaphore_wait(barrier, len(greeted))
     y_copies = [
         pltpu.make_async_remote_copy(src_ref=src, dst_ref=dst, send_sem=send_sems.at[i], recv_sem=recv_sems.at[i],
@@ -311,6 +344,9 @@
     ]
     for copy in y_copies:
         copy.start()
+    for t in range(1, tiles - 1):
+        loads[t].wait()
+    first.prepare(0)
     first.send(0)
     first.prepare(1)
     first.send(1)
@@ -326,23 +362,24 @@
     first.send(2)
     for c in range(3):
         first.receive(c)
-    first.all_lines([0], approx_four)
+    first.lines([0], approx_four)
 
     second.prepare(0)
     second.send(0)
-    first.all_lines([1, 2, 3])
+    for band in (1, 2, 3):
+        first.lines([band])
     second.receive(0)
-    second.all_lines([0], approx_five)
+    second.lines([0], approx_five)
 
     third.prepare(0)
     third.send(0)
-    second.all_lines([1, 2, 3])
+    second.lines([1, 2, 3])
     third.receive(0)
-    third.all_lines([0, 1, 2, 3], approx_ref)
+    third.lines([0, 1, 2, 3], approx_ref)
 
     for copy in y_copies:
         copy.wait_send()
-    for level in levels:
+    for level in (first, second, third):
         for copies in level.copies:
             for copy in copies:
                 copy.wait_send()
@@ -357,7 +394,7 @@
         tiles = ny // LANES
         shapes = [(7, z // 2, x // 2, p * LANES) for z, x, p in sizes]
         shapes.append(shapes[-1][1:])
-        n_sems = 2 + 8 * 5
+        n_sems = 42
         packed = (nz * nx * HALO // LANES, LANES)
         scratch = [
             pltpu.SemaphoreType.DMA((n_sems,)),

time: 29.6 us -> 28.4 us (0.959)
  Pallas kernels: 28.5 us -> 27.3 us
    pallas_call x1, Pallas kernels: 27.5 us -> 26.3 us  [on_device(): pl.pallas_call(functools.partial(kernel, sizes, axes), out_shape=[pltpu.V...]
where the time goes in v8:
time: 28.4 us; the launch traced here: 27.9 us
  Pallas kernels  27.3 us (96%)
  between operations  0.64 us (2%)
    pallas_call x1, Pallas kernels, on_device(): pl.pallas_call(functools.partial(kernel, sizes, axes), out_shape=[pltpu.V...  26.3 us
    pallas_call x1, Pallas kernels, on_device(): pl.pallas_call(hand_out, out_shape=outs, in_specs=[pl.BlockSpec(memory_sp...  0.99 us

profile of v8, /device:TPU:0, one launch (start us, length us, event | category | flops | bytes accessed | tf_op | source)
XLA Modules:
  0.0 27.9 jit_solution(15432337502578902298)
XLA Ops:
  0.6 26.3 %shard_map.46 = (f32[7,8,8,512]{3,2,1,0:T(8,128)S(1)}, f32[7,4,4,256]{3,2,1,0:T(4,128)S(1)}, f32[7,2,2,128]{3,2,1,0:T(2,128)S(1)}, f32[2,2,128]{2,1,0:T(2,128)S(1)}) custom-call(f32[16,16,1024]{2,1,0:T(8,128)} %u_ref.1), custom_call_target="tpu_custom_call" | custom-call | flops 20000000 | bytes 2097152 | tf_op jit(solution)/shard_map/pallas_call | solution.py:411
  27.0 1.0 %shard_map.47 = (f32[7,8,8,512]{3,2,1,0:T(8,128)}, f32[7,4,4,256]{3,2,1,0:T(4,128)}, f32[7,2,2,128]{3,2,1,0:T(2,128)}, f32[2,2,128]{2,1,0:T(2,128)}) custom-call(f32[7,8,8,512]{3,2,1,0:T(8,128)S(1)} %get-tuple-element.8.refs_0_, f32[7,4,4,256]{3,2,1,0:T(4,128)S(1)} %get-tuple-element.9.refs_1_, f32[7,2,2,128]{3,2,1,0:T(2,128)S(1)} %get-tuple-element.10.refs_2_, ...), custom_call_target="tpu_custom_call" | custom-call | bytes 2097152 | tf_op jit(solution)/shard_map/pallas_call | solution.py:422

commit v9 on v8

--- a/solution.py
+++ b/solution.py
@@ -344,10 +344,12 @@
     ]
     for copy in y_copies:
         copy.start()
-    for t in range(1, tiles - 1):
+    for t in range(1, 2 * half):
         loads[t].wait()
     first.prepare(0)
     first.send(0)
+    for t in range(2 * half, tiles - 1):
+        loads[t].wait()
     first.prepare(1)
     first.send(1)
     for copy in y_copies:

time: 28.4 us -> 28.4 us (level)
  no operation moved by 1% of the time
where the time goes in v9:
time: 28.4 us; the launch traced here: 27.9 us
  Pallas kernels  27.3 us (96%)
  between operations  0.64 us (2%)
    pallas_call x1, Pallas kernels, on_device(): pl.pallas_call(functools.partial(kernel, sizes, axes), out_shape=[pltpu.V...  26.3 us
    pallas_call x1, Pallas kernels, on_device(): pl.pallas_call(hand_out, out_shape=outs, in_specs=[pl.BlockSpec(memory_sp...  0.99 us

profile of v9, /device:TPU:0, one launch (start us, length us, event | category | flops | bytes accessed | tf_op | source)
XLA Modules:
  0.0 27.9 jit_solution(6529189057308570432)
XLA Ops:
  0.6 26.3 %shard_map.46 = (f32[7,8,8,512]{3,2,1,0:T(8,128)S(1)}, f32[7,4,4,256]{3,2,1,0:T(4,128)S(1)}, f32[7,2,2,128]{3,2,1,0:T(2,128)S(1)}, f32[2,2,128]{2,1,0:T(2,128)S(1)}) custom-call(f32[16,16,1024]{2,1,0:T(8,128)} %u_ref.1), custom_call_target="tpu_custom_call" | custom-call | flops 20000000 | bytes 2097152 | tf_op jit(solution)/shard_map/pallas_call | solution.py:413
  26.9 1.0 %shard_map.47 = (f32[7,8,8,512]{3,2,1,0:T(8,128)}, f32[7,4,4,256]{3,2,1,0:T(4,128)}, f32[7,2,2,128]{3,2,1,0:T(2,128)}, f32[2,2,128]{2,1,0:T(2,128)}) custom-call(f32[7,8,8,512]{3,2,1,0:T(8,128)S(1)} %get-tuple-element.8.refs_0_, f32[7,4,4,256]{3,2,1,0:T(4,128)S(1)} %get-tuple-element.9.refs_1_, f32[7,2,2,128]{3,2,1,0:T(2,128)S(1)} %get-tuple-element.10.refs_2_, ...), custom_call_target="tpu_custom_call" | custom-call | bytes 2097152 | tf_op jit(solution)/shard_map/pallas_call | solution.py:424

commit v10 on v9

--- a/solution.py
+++ b/solution.py
@@ -309,7 +309,7 @@
     for where in greeted:
         pl.semaphore_signal(barrier, inc=1, device_id=where, device_id_type=MESH)
 
-    half = pairs // 2
+    half = pairs - 1
     sems = (send_sems, recv_sems)
     chunks = [(0, half), (half, pairs), (pairs, pairs + 1)]
     source = raw.reshape(tiles + 1, nz * nx, LANES)

time: 28.4 us -> 28.6 us (level)
  no operation moved by 1% of the time
where the time goes in v10:
time: 28.6 us; the launch traced here: 28.1 us
  Pallas kernels  27.5 us (96%)
  between operations  0.64 us (2%)
    pallas_call x1, Pallas kernels, on_device(): pl.pallas_call(functools.partial(kernel, sizes, axes), out_shape=[pltpu.V...  26.5 us
    pallas_call x1, Pallas kernels, on_device(): pl.pallas_call(hand_out, out_shape=outs, in_specs=[pl.BlockSpec(memory_sp...  0.99 us

profile of v10, /device:TPU:0, one launch (start us, length us, event | category | flops | bytes accessed | tf_op | source)
XLA Modules:
  0.0 28.1 jit_solution(15823237603624485606)
XLA Ops:
  0.6 26.5 %shard_map.46 = (f32[7,8,8,512]{3,2,1,0:T(8,128)S(1)}, f32[7,4,4,256]{3,2,1,0:T(4,128)S(1)}, f32[7,2,2,128]{3,2,1,0:T(2,128)S(1)}, f32[2,2,128]{2,1,0:T(2,128)S(1)}) custom-call(f32[16,16,1024]{2,1,0:T(8,128)} %u_ref.1), custom_call_target="tpu_custom_call" | custom-call | flops 20000000 | bytes 2097152 | tf_op jit(solution)/shard_map/pallas_call | solution.py:413
  27.2 1.0 %shard_map.47 = (f32[7,8,8,512]{3,2,1,0:T(8,128)}, f32[7,4,4,256]{3,2,1,0:T(4,128)}, f32[7,2,2,128]{3,2,1,0:T(2,128)}, f32[2,2,128]{2,1,0:T(2,128)}) custom-call(f32[7,8,8,512]{3,2,1,0:T(8,128)S(1)} %get-tuple-element.8.refs_0_, f32[7,4,4,256]{3,2,1,0:T(4,128)S(1)} %get-tuple-element.9.refs_1_, f32[7,2,2,128]{3,2,1,0:T(2,128)S(1)} %get-tuple-element.10.refs_2_, ...), custom_call_target="tpu_custom_call" | custom-call | bytes 2097152 | tf_op jit(solution)/shard_map/pallas_call | solution.py:424
